TPU v7x, 256 devices: a whole 4x4x8 slice. The times are simulated.
256 devices in a mesh: ctx: 32 (over x_lo, z, core), tp: 8 (over y, x_hi).
Axes of the slice: x: 4 (x_hi: 2, x_lo: 2; x = x_hi * 2 + x_lo), y: 4, z: 8, core: 2. Of those that a mesh axis runs over, the one named last changes fastest.
Arguments:
- query: bfloat16 [24576, 4096], P('ctx', 'tp'), may hold values from -36 to 36
- key: bfloat16 [24576, 1024], P('ctx', 'tp'), may hold values from -32 to 32
- value: bfloat16 [24576, 1024], P('ctx', 'tp'), may hold values from -6 to 6
- keep_rank: int32 [32, 768], P('ctx'), may hold values from 0 to 767, each once within a row
- kept_count: int32 [32], replicated, may hold values from 1 to 768, 12288 in all
- out_weight: bfloat16 [4096, 8192], P('tp'), may hold values from -0.09375 to 0.09375
Outputs:
- mixed: bfloat16 [12288, 8192], P('ctx', 'tp')
Inputs may be any that keep to these rules, and one draw needn't show every extreme that they name: `keep_rank`: each row is a permutation of 0 to 767. `kept_count`: the counts sum to 12288; the largest is exactly 768.
All inputs are finite; a program needn't handle non-finite values.
Results may differ from a plain program's by a relative error of at most 0.019.
The roundings to bfloat16 on the way count: a program that leaves them out, or rounds other values in their place, can miss the bound.
Values may be sent and summed in bfloat16 or wider, within the bound.
A program may use at most 128 MiB of HBM per device.

v0:
```python
import math

import jax
import jax.numpy as jnp
from jax import lax
from jax.sharding import PartitionSpec as P

HD = 128
TOK_DEV = 384


rope_base = 1000000.0
masked_score = -1e30


def rotate(rows, positions):
    count_rows = rows.shape[0]
    heads = rows.shape[1] // HD
    half_dim = HD // 2
    as_float = rows.astype(jnp.float32).reshape(count_rows, heads, HD)
    inv_freq = rope_base ** (-(jnp.arange(half_dim, dtype=jnp.float32) * 2.0 / HD))
    angles = positions.astype(jnp.float32)[:, None] * inv_freq[None, :]
    cosine = jnp.cos(angles)[:, None, :]
    sine = jnp.sin(angles)[:, None, :]
    first_half = as_float[..., :half_dim]
    second_half = as_float[..., half_dim:]
    turned = jnp.concatenate(
        [first_half * cosine - second_half * sine, second_half * cosine + first_half * sine],
        axis=-1,
    )
    return turned.reshape(count_rows, heads * HD).astype(jnp.bfloat16)


def local(query, key, value, keep_rank, kept_count, out_weight):
    ctx_size = lax.axis_size("ctx")
    my_shard = lax.axis_index("ctx")
    orig_rows = query.shape[0]
    slot_cap = orig_rows // ctx_size
    rows_dev = TOK_DEV
    shard_ids = jnp.arange(ctx_size, dtype=jnp.int32)
    count_ends = jnp.cumsum(kept_count)
    count_starts = count_ends - kept_count
    my_count = jnp.sum(jnp.where(shard_ids == my_shard, kept_count, 0))
    my_start = jnp.sum(jnp.where(shard_ids == my_shard, count_starts, 0))
    local_rows = jnp.arange(orig_rows, dtype=jnp.int32)
    positions = my_shard * orig_rows + local_rows
    rot_query = rotate(query, positions)
    rot_key = rotate(key, positions)
    is_kept = keep_rank[0] < my_count
    kept_order = jnp.cumsum(is_kept.astype(jnp.int32)) - 1
    kept_rows = (
        jnp.zeros((orig_rows,), jnp.int32)
        .at[jnp.where(is_kept, kept_order, orig_rows)]
        .set(local_rows, mode="drop")
    )
    dest_ids = shard_ids[:, None]
    slot_ids = jnp.arange(slot_cap, dtype=jnp.int32)[None, :]
    first_slot = (my_start - dest_ids + ctx_size - 1) // ctx_size
    offsets = (first_slot + slot_ids) * ctx_size + dest_ids - my_start
    is_valid = (offsets < my_count).reshape(-1)
    picked = kept_rows[jnp.clip(offsets, 0, orig_rows - 1).reshape(-1)]

    def pack_rows(source_rows):
        return jnp.where(is_valid[:, None], source_rows[picked], jnp.zeros((), source_rows.dtype))

    got_query, got_key, got_value = (
        lax.all_to_all(pack_rows(rot_query), "ctx", split_axis=0, concat_axis=0, tiled=True),
        lax.all_to_all(pack_rows(rot_key), "ctx", split_axis=0, concat_axis=0, tiled=True),
        lax.all_to_all(pack_rows(value), "ctx", split_axis=0, concat_axis=0, tiled=True),
    )
    own_slots = jnp.arange(rows_dev, dtype=jnp.int32)
    query_glob = own_slots * ctx_size + my_shard
    sources = jnp.sum((count_ends[None, :] <= query_glob[:, None]).astype(jnp.int32), axis=1)
    source_start = jnp.sum(
        jnp.where(shard_ids[None, :] == sources[:, None], count_starts[None, :], 0), axis=1
    )
    slot_of = own_slots - (source_start - my_shard + ctx_size - 1) // ctx_size
    places = sources * slot_cap + slot_of
    query_local = got_query[places]
    key_local = got_key[places]
    value_local = got_value[places]
    heads_dev = query_local.shape[1] // HD
    kv_dev = key_local.shape[1] // HD
    group_size = heads_dev // kv_dev
    queries = query_local.reshape(rows_dev, kv_dev, group_size, HD)

    def absorb_block(state, key_block, value_block, first_row):
        run_max, run_sum, run_acc = state
        block_len = key_block.shape[0]
        whole_rows = first_row + jnp.arange(block_len, dtype=jnp.int32)
        key_glob = whole_rows % rows_dev * ctx_size + whole_rows // rows_dev
        allowed = key_glob[None, :] <= query_glob[:, None]
        key_heads = key_block.reshape(block_len, kv_dev, HD)
        value_heads = value_block.reshape(block_len, kv_dev, HD)
        scores = jnp.einsum(
            "rkgd,pkd->kgrp", queries, key_heads, preferred_element_type=jnp.float32
        ) / math.sqrt(HD)
        scores = jnp.where(allowed, scores, masked_score)
        new_max = jnp.maximum(run_max, jnp.max(scores, axis=-1))
        weights = jnp.where(allowed, jnp.exp(scores - new_max[..., None]), 0.0)
        rescale = jnp.exp(run_max - new_max)
        new_sum = run_sum * rescale + jnp.sum(weights, axis=-1)
        weights_b = weights.astype(jnp.bfloat16)
        new_acc = run_acc * rescale[..., None] + jnp.einsum(
            "kgrp,pkd->kgrd", weights_b, value_heads, preferred_element_type=jnp.float32
        )
        return (new_max, new_sum, new_acc)

    start_state = (
        jnp.full((kv_dev, group_size, rows_dev), masked_score, jnp.float32),
        jnp.zeros((kv_dev, group_size, rows_dev), jnp.float32),
        jnp.zeros((kv_dev, group_size, rows_dev, HD), jnp.float32),
    )
    state = start_state
    key_piece = lax.all_gather(key_local, "ctx", axis=0, tiled=True)
    value_piece = lax.all_gather(value_local, "ctx", axis=0, tiled=True)
    total_rows = key_piece.shape[0]
    step_rows = 512
    turns = total_rows // step_rows
    key_blocks = key_piece.reshape(turns, step_rows, key_piece.shape[1])
    value_blocks = value_piece.reshape(turns, step_rows, value_piece.shape[1])
    block_firsts = jnp.arange(turns, dtype=jnp.int32) * step_rows

    def one_turn(inner, item):
        key_block, value_block, block_first = item
        return (absorb_block(inner, key_block, value_block, block_first), None)

    state, _ = lax.scan(one_turn, state, (key_blocks, value_blocks, block_firsts))
    run_max, run_sum, run_acc = state
    attention = (
        jnp.transpose(run_acc / run_sum[..., None], (2, 0, 1, 3))
        .reshape(rows_dev, heads_dev * HD)
        .astype(jnp.bfloat16)
    )
    summed = lax.psum_scatter(
        lax.dot_general(
            out_weight, attention, (((0,), (1,)), ((), ())), preferred_element_type=jnp.float32
        ).astype(jnp.bfloat16),
        "tp",
        scatter_dimension=0,
        tiled=True,
    ).astype(jnp.float32)
    projected = jnp.transpose(summed).astype(jnp.bfloat16)
    received = lax.all_to_all(projected, "ctx", split_axis=0, concat_axis=0, tiled=True)
    return jnp.transpose(
        received.reshape(ctx_size, rows_dev // ctx_size, received.shape[1]), (1, 0, 2)
    ).reshape(rows_dev, received.shape[1])


def solution(mesh):
    placed = (P("ctx", "tp"), P("ctx", "tp"), P("ctx", "tp"), P("ctx", None), P(), P("tp", None))
    return jax.shard_map(
        local, mesh=mesh, in_specs=placed, out_specs=P("ctx", "tp"), check_vma=False
    )
```

profile of v0, /device:TPU:1, one launch (start us, length us, event | category | flops | bytes accessed | tf_op | source)
XLA Modules:
  0.0 552.0 jit_solution(12416440801180032782)
XLA Ops:
  15.2 3.4 scatter_custom_fusion
  18.6 3.2 gather_fusion
  23.1 1.9 gather_fusion.1
  24.9 1.9 gather_fusion.5
  27.7 11.0 %all-to-all-start.2 = ((bf16[32,24,128]{2,1,0:T(8,128)(2,1)}), bf16[32,24,128]{2,1,0:T(8,128)(2,1)S(1)}, u32[]{:S(2)}, u32[]{:S(2)}) async-start(bf16[32,24,128]{2,1,0:T(8,128)(2,1)} %get-tuple-element.232), calls=%async_computation.2 | async-start | bytes 393216 | tf_op jit(solution)/shard_map/all_to_all | solution.py:69
  39.0 9.9 %all-to-all-done.2 = bf16[32,24,128]{2,1,0:T(8,128)(2,1)S(1)} async-done(((bf16[32,24,128]{2,1,0:T(8,128)(2,1)}), bf16[32,24,128]{2,1,0:T(8,128)(2,1)S(1)}, u32[]{:S(2)}, u32[]{:S(2)}) %all-to-all-start.2) | async-done | bytes 196640 | tf_op jit(solution)/shard_map/all_to_all | solution.py:69
  48.9 1.9 gather_fusion.6
  50.9 14.8 %all_to_all.36 = bf16[32,24,128]{2,1,0:T(8,128)(2,1)S(1)} all-to-all(bf16[32,24,128]{2,1,0:T(8,128)(2,1)S(1)} %get-tuple-element.233), channel_id=1, replica_groups=mesh['ctx'=32,'tp'=8] {'ctx'}, dimensions={0} | all-to-all | bytes 393216 | tf_op jit(solution)/shard_map/all_to_all | solution.py:68
  65.7 1.9 gather_fusion.2
  72.2 2.7 gather_fusion.3
  76.0 5.4 all-to-all-start.1
  82.2 26.0 %all-to-all-done.1 = bf16[32,24,512]{2,1,0:T(8,128)(2,1)S(1)} async-done(((bf16[32,24,512]{2,1,0:T(8,128)(2,1)}), bf16[32,24,512]{2,1,0:T(8,128)(2,1)S(1)}, u32[]{:S(2)}, u32[]{:S(2)}) %all-to-all-start.1) | async-done | bytes 786464 | tf_op jit(solution)/shard_map/all_to_all | solution.py:67
  108.1 2.1 gather_fusion.4
  111.1 9.4 %all-gather.7.cloned.1.call-done = bf16[12288,128]{1,0:T(8,128)(2,1)} async-done(((bf16[384,128]{1,0:T(8,128)(2,1)}), bf16[12288,128]{1,0:T(8,128)(2,1)}) %all-gather.7.cloned.1.call-update) | async-done | bytes 3145744 | tf_op jit(solution)/shard_map/all_gather | solution.py:116
  120.5 67.6 %all-gather.5.cloned.1.call-done = bf16[12288,128]{1,0:T(8,128)(2,1)} async-done(((bf16[384,128]{1,0:T(8,128)(2,1)}), bf16[12288,128]{1,0:T(8,128)(2,1)}) %all-gather.5.cloned.1.call-update) | async-done | bytes 3145744 | tf_op jit(solution)/shard_map/all_gather | solution.py:115
  188.1 206.0 %while.17 = (s32[]{:T(128)}, f32[1,4,384]{2,1,0:T(4,128)S(1)}, f32[1,4,384]{2,1,0:T(4,128)}, f32[1,4,384,128]{3,2,1,0:T(8,128)}, s32[24]{0:T(128)}, /*index=5*/b...) while((s32[]{:T(128)}, f32[1,4,384]{2,1,0:T(4,128)S(1)}, ...), condition=%wide.region_11.12_spmd.clone, body=%wide.region_8.11_spmd.clone.sunk | while | flops 413680896 | bytes 12607685 | solution.py:128
  190.3 1.7 fusion.66
  192.1 2.9 fusion.69
  198.6 1.7 fusion.66
  200.4 3.3 fusion.69
  207.2 1.7 fusion.66
  209.0 3.3 fusion.69
  215.8 1.7 fusion.66
  217.5 3.3 fusion.69
  224.4 1.7 fusion.66
  226.1 3.3 fusion.69
  233.0 1.7 fusion.66
  234.7 3.3 fusion.69
  241.6 1.7 fusion.66
  243.3 3.3 fusion.69
  250.2 1.7 fusion.66
  251.9 3.3 fusion.69
  258.8 1.7 fusion.66
  260.5 3.3 fusion.69
  267.4 1.7 fusion.66
  269.1 3.3 fusion.69
  275.9 1.7 fusion.66
  277.7 3.3 fusion.69
  284.5 1.7 fusion.66
  286.3 3.3 fusion.69
  293.1 1.7 fusion.66
  294.9 3.3 fusion.69
  303.5 3.3 fusion.69
  310.3 1.7 fusion.66
  312.1 3.3 fusion.69
  318.9 1.7 fusion.66
  320.7 3.3 fusion.69
  327.5 1.7 fusion.66
  329.3 3.3 fusion.69
  337.9 3.3 fusion.69
  344.7 1.7 fusion.66
  346.5 3.3 fusion.69
  353.3 1.7 fusion.66
  355.1 3.3 fusion.69
  361.9 1.7 fusion.66
  363.7 3.3 fusion.69
  372.3 3.3 fusion.69
  379.1 1.7 fusion.66
  380.9 3.3 fusion.69
  387.7 1.7 fusion.66
  389.5 3.3 fusion.69
  396.3 9.5 %fusion.34 = bf16[8192,384]{0,1:T(8,128)(2,1)} fusion(bf16[384,512]{0,1:T(8,128)(2,1)S(1)} %bitcast.127, bf16[512,8192]{1,0:T(8,128)(2,1)} %param.13), kind=kOutput, calls=%fused_computation.50 | convolution fusion | flops 3224371200 | bytes 15073280 | tf_op jit(solution)/shard_map/dot_general | solution.py:136
  405.8 102.4 %reduce-scatter.2.cloned.1.call-done = bf16[1024,384]{0,1:T(8,128)(2,1)} async-done(((bf16[8192,384]{0,1:T(8,128)(2,1)}), bf16[1024,384]{0,1:T(8,128)(2,1)}) %reduce-scatter.2.cloned.1.call-update) | async-done | bytes 786448 | tf_op jit(solution)/shard_map/reduce_scatter | solution.py:135
  509.5 34.7 %all_to_all.37 = bf16[32,12,1024]{2,1,0:T(8,128)(2,1)S(1)} all-to-all(bf16[32,12,1024]{2,1,0:T(8,128)(2,1)S(1)} %all_to_all.30), channel_id=1, replica_groups=mesh['ctx'=32,'tp'=8] {'ctx'}, dimensions={0} | all-to-all | bytes 1572864 | tf_op jit(solution)/shard_map/all_to_all | solution.py:144
  (353 shorter events, 113.1 us)
Async XLA Ops:
  6.5 18.4 %copy-start = (bf16[768,128]{1,0:T(8,128)(2,1)S(1)}, bf16[768,128]{1,0:T(8,128)(2,1)}, u32[]{:S(2)}) copy-start(bf16[768,128]{1,0:T(8,128)(2,1)} %param.10) | copy-start | bytes 589828
  6.5 15.3 %copy-start.4 = (bf16[768,128]{1,0:T(8,128)(2,1)S(1)}, bf16[768,128]{1,0:T(8,128)(2,1)}, u32[]{:S(2)}) copy-start(bf16[768,128]{1,0:T(8,128)(2,1)} %param.9) | copy-start | bytes 589828
  23.0 44.6 %copy-start.1 = (bf16[768,512]{1,0:T(8,128)(2,1)S(1)}, bf16[768,512]{1,0:T(8,128)(2,1)}, u32[]{:S(2)}) copy-start(bf16[768,512]{1,0:T(8,128)(2,1)} %param.8) | copy-start | bytes 2359300
  27.7 21.3 %all-to-all-start.2 = ((bf16[32,24,128]{2,1,0:T(8,128)(2,1)}), bf16[32,24,128]{2,1,0:T(8,128)(2,1)S(1)}, u32[]{:S(2)}, u32[]{:S(2)}) async-start(bf16[32,24,128]{2,1,0:T(8,128)(2,1)} %get-tuple-element.232), calls=%async_computation.2 | async-start | bytes 393216 | tf_op jit(solution)/shard_map/all_to_all | solution.py:69
  38.7 81.8 %all-gather.7.cloned.1.call-start = ((), (), s32[]{:S(2)}) async-start(), calls=%async_computation.7 | async-start | bytes 3244032 | tf_op jit(solution)/shard_map/all_gather | solution.py:116
  50.9 137.3 %all-gather.5.cloned.1.call-start = ((), (), s32[]{:S(2)}) async-start(), calls=%async_computation.6 | async-start | bytes 3244032 | tf_op jit(solution)/shard_map/all_gather | solution.py:115
  76.0 32.2 %all-to-all-start.1 = ((bf16[32,24,512]{2,1,0:T(8,128)(2,1)}), bf16[32,24,512]{2,1,0:T(8,128)(2,1)S(1)}, u32[]{:S(2)}, u32[]{:S(2)}) async-start(bf16[32,24,512]{2,1,0:T(8,128)(2,1)} %broadcast_select_fusion), calls=%async_computation.1 | async-start | bytes 1572864 | tf_op jit(solution)/shard_map/all_to_all | solution.py:67
  81.4 426.9 %reduce-scatter.2.cloned.1.call-start = ((), (), s32[]{:S(2)}) async-start(), calls=%async_computation.5 | async-start | bytes 7077888 | tf_op jit(solution)/shard_map/reduce_scatter | solution.py:135
  195.0 0.8 copy-start.2
  195.8 0.6 copy-start.3
  203.6 0.8 copy-start.2
  204.4 0.6 copy-start.3
  212.2 0.8 copy-start.2
  213.0 0.6 copy-start.3
  220.8 0.8 copy-start.2
  221.6 0.6 copy-start.3
  229.4 0.8 copy-start.2
  230.2 0.6 copy-start.3
  238.0 0.8 copy-start.2
  238.8 0.6 copy-start.3
  246.6 0.8 copy-start.2
  247.4 0.6 copy-start.3
  255.2 0.8 copy-start.2
  256.0 0.6 copy-start.3
  263.8 0.8 copy-start.2
  264.6 0.6 copy-start.3
  272.4 0.8 copy-start.2
  273.2 0.6 copy-start.3
  281.0 0.8 copy-start.2
  281.8 0.6 copy-start.3
  289.6 0.8 copy-start.2
  290.4 0.6 copy-start.3
  298.2 0.8 copy-start.2
  299.0 0.6 copy-start.3
  306.8 0.8 copy-start.2
  307.6 0.6 copy-start.3
  315.4 0.8 copy-start.2
  316.2 0.6 copy-start.3
  324.0 0.8 copy-start.2
  324.8 0.6 copy-start.3
  332.5 0.8 copy-start.2
  333.4 0.6 copy-start.3
  341.1 0.8 copy-start.2
  342.0 0.6 copy-start.3
  349.7 0.8 copy-start.2
  350.6 0.6 copy-start.3
  358.3 0.8 copy-start.2
  359.1 0.6 copy-start.3
  366.9 0.8 copy-start.2
  367.7 0.6 copy-start.3
  375.5 0.8 copy-start.2
  376.3 0.6 copy-start.3
  384.1 0.8 copy-start.2
  384.9 0.6 copy-start.3
  392.7 0.8 copy-start.2
  393.5 0.6 copy-start.3
Sparse Core Ops, SparseCore 0:
  51.0 69.5 all-gather.6
  122.4 65.7 all-gather.4
  405.9 102.2 reduce-scatter.1
where the time goes:
time: 555 us; the launch traced here: 552 us
  waiting for transfers between devices  215 us (39%)
  matrix products  129 us (23%)
  local copies, waits for them, and re-layouts  70 us (13%)
  other arithmetic  56.3 us (10%)
  blocking collectives  49.5 us (9%)
  starting transfers between devices  16.8 us (3%)
  between operations  13.4 us (2%)
    reduce_scatter x1, waiting for transfers between devices, local(): lax.psum_scatter(lax.dot_general(out_weight, attention, (((0,), (1,)), ((...  102 us
    dot_general x24, matrix products, absorb_block(): jnp.einsum('kgrp,pkd->kgrd', weights_b, value_heads, preferred_element_ty...  77.7 us
    all_gather x1, waiting for transfers between devices, local(): key_piece = lax.all_gather(key_local, 'ctx', axis=0, tiled=True)  67.6 us
    dot_general x24, matrix products, absorb_block(): jnp.einsum('rkgd,pkd->kgrp', queries, key_heads, preferred_element_type=j...  41.9 us
    all_to_all x1, blocking collectives, local(): lax.all_to_all(projected, 'ctx', split_axis=0, concat_axis=0, tiled=True)  34.7 us
    dynamic_slice x24, local copies, waits for them, and re-layouts, local(): lax.scan(one_turn, state, (key_blocks, value_blocks, block_firsts))  30.4 us
    all_to_all x1, waiting for transfers between devices, local(): lax.all_to_all(pack_rows(rot_query), 'ctx', split_axis=0, concat_axis=0,...  26 us
    reduce_sum x24, other arithmetic, absorb_block(): new_sum = run_sum * rescale + jnp.sum(weights, axis=-1)  18.8 us
  transfers between devices with their start and end apart: 5, of which 5 were waited for; matrix products, arithmetic and copies ran while one was open for 3% of the time, Pallas kernels for 0%

commit v1 on v0

v1 whole, which is shorter than its diff:
```python
import functools
import math

import jax
import jax.numpy as jnp
import numpy as np
from jax import lax
from jax.experimental import pallas as pl
from jax.experimental.pallas import tpu as pltpu
from jax.sharding import PartitionSpec as P

HD = 128
ROWS = 768
BLK = 48
CHIPS = 16
SHARDS = 32
KEPT = 12288
MESH = pl.DeviceIdType.MESH
VMEM = pltpu.VMEM
BF = jnp.bfloat16
F32 = jnp.float32


def tables():
    freq = 1000000.0 ** (-(np.arange(HD // 2) * 2.0 / HD))
    sign = np.concatenate([-np.ones(HD // 2), np.ones(HD // 2)])
    both = np.concatenate([freq, freq])
    own = np.arange(ROWS)[:, None] * both
    base = (np.arange(SHARDS) * ROWS)[:, None] * both
    col = np.arange(SHARDS * BLK)
    cols = np.zeros((8, SHARDS * BLK), np.int32)
    cols[0], cols[1] = col // BLK, col % BLK
    f = lambda a: a.astype(np.float32)
    return (f(np.cos(own)), f(np.sin(own) * sign), f(np.cos(base)), f(np.sin(base) * sign), cols)


def place():
    c, t = lax.axis_index("ctx"), lax.axis_index("tp")
    return dict(c=c, t=t, core=c % 2, z=(c // 2) % 8, xl=c // 16, j=c // 2, y=t // 2, xh=t % 2)


def ctx_of(xl, z, core):
    return xl * 16 + z * 2 + core


def remote(src, dst, ssem, rsem, dev):
    return pltpu.make_async_remote_copy(
        src_ref=src, dst_ref=dst, send_sem=ssem, recv_sem=rsem, device_id=dev, device_id_type=MESH)


def exchange_kernel(cnt, rank, q, k, v, ci, si, cb, sb, cols, w,
                    qo, kv, wf,
                    xs, sq, skv, rq, rkv, unp,
                    kv_s, kv_r, q_s, q_r, ring_s, ring_r, die_r, w_s, w_r, wd_s, wd_r, loc):
    me = place()
    c, t, core, z, xl, j, y, xh = (me[n] for n in ("c", "t", "core", "z", "xl", "j", "y", "xh"))
    bar = pltpu.get_barrier_semaphore()

    def hail(i, _):
        pl.semaphore_signal(bar, inc=1, device_id=((c + i) % SHARDS, t), device_id_type=MESH)
        return 0
    lax.fori_loop(1, SHARDS, hail, 0)
    cx = ctx_of(1 - xl, z, core)
    w_peers = [(c, ((y + d) % 4) * 2 + xh) for d in (1, 2, 3)]
    w_peers += [(cx, ((y + d) % 4) * 2 + (1 - xh)) for d in (0, 1, 2, 3)]
    for peer in w_peers:
        pl.semaphore_signal(bar, inc=1, device_id=peer, device_id_type=MESH)

    cbr, sbr = cb[pl.ds(c, 1), :], sb[pl.ds(c, 1), :]
    civ, siv = ci[...], si[...]
    cosv = civ * cbr - siv * sbr
    sinv = siv * cbr + civ * sbr
    scale = math.log2(math.e) / math.sqrt(HD)
    for h in range(5):
        src = k[...] if h == 4 else q[:, h * HD:(h + 1) * HD]
        x = src.astype(F32)
        out = x * cosv + pltpu.roll(x, HD // 2, 1) * sinv
        if h < 4:
            out = out * scale
        xs[:, h * HD:(h + 1) * HD] = out.astype(BF)
    xs[:, 5 * HD:] = v[...]

    my_count = cnt[c]
    start = jnp.int32(0)
    for s in range(SHARDS):
        start = start + jnp.where(s < c, cnt[s], 0)
    kept = rank[...] < my_count
    keptf = jnp.where(kept, 1.0, 0.0).astype(BF)
    i0 = lax.broadcasted_iota(jnp.int32, (ROWS, ROWS), 0)
    i1 = lax.broadcasted_iota(jnp.int32, (ROWS, ROWS), 1)
    tri = jnp.where(i0 < i1, 1.0, 0.0).astype(BF)
    order = jnp.dot(jnp.broadcast_to(keptf, (16, ROWS)), tri, preferred_element_type=F32)[0:1]
    slot = order.astype(jnp.int32) + lax.rem(start, jnp.int32(ROWS))
    slot = jnp.where(slot >= ROWS, slot - ROWS, slot)
    slot = jnp.where(kept, slot, -1)
    perm = jnp.where(i0 == slot, 1.0, 0.0).astype(BF)
    kvp = jnp.dot(perm, xs[:, 4 * HD:], preferred_element_type=F32).astype(BF)
    skv[0] = kvp[:, :HD]
    skv[1] = kvp[:, HD:]

    pl.semaphore_wait(bar, SHARDS - 1 + 7)

    def kv_copy(d):
        dj = d // 2
        return remote(skv.at[d % 2, pl.ds(pl.multiple_of(dj * BLK, BLK), BLK)],
                      rkv.at[pl.ds(pl.multiple_of(c * BLK, BLK), BLK)],
                      kv_s.at[d], kv_r.at[c], (d, t))

    def q_copy(d):
        dj = d // 2
        return remote(sq.at[d % 2, pl.ds(pl.multiple_of(dj * BLK, BLK), BLK)],
                      rq.at[pl.ds(pl.multiple_of(c * BLK, BLK), BLK)],
                      q_s.at[d], q_r.at[c], (d, t))

    def start_kv(i, _):
        kv_copy((c + i) % SHARDS).start()
        return 0
    lax.fori_loop(1, SHARDS, start_kv, 0)
    own_rows = pl.ds(pl.multiple_of(j * BLK, BLK), BLK)
    to_rows = pl.ds(pl.multiple_of(c * BLK, BLK), BLK)
    own_kv = pltpu.make_async_copy(skv.at[core, own_rows], rkv.at[to_rows], loc.at[0])
    own_kv.start()

    half = 256

    def w_copy(n):
        peer = w_peers[n]
        return remote(w.at[pl.ds(pl.multiple_of(core * half, half), half),
                           pl.ds(pl.multiple_of(peer[1] * 1024, 1024), 1024)],
                      wf.at[pl.ds(pl.multiple_of(t * 512 + core * half, half), half)],
                      w_s.at[n], w_r.at[t], peer)
    for n in range(7):
        w_copy(n).start()
    w_own = pltpu.make_async_copy(
        w.at[:, pl.ds(pl.multiple_of(t * 1024, 1024), 1024)],
        wf.at[pl.ds(pl.multiple_of(t * 512, 512), 512)], loc.at[2])
    w_own.start()

    qp = jnp.dot(perm, xs[:, :4 * HD], preferred_element_type=F32).astype(BF)
    sq[0] = qp[:, :2 * HD]
    sq[1] = qp[:, 2 * HD:]

    def start_q(i, _):
        q_copy((c + i) % SHARDS).start()
        return 0
    lax.fori_loop(1, SHARDS, start_q, 0)
    own_q = pltpu.make_async_copy(sq.at[core, own_rows], rq.at[to_rows], loc.at[1])
    own_q.start()

    grp, mod = cols[0:1, :], cols[1:2, :]
    first = jnp.zeros((1, SHARDS * BLK), jnp.int32)
    last = jnp.zeros((1, SHARDS * BLK), jnp.int32)
    for s in range(SHARDS):
        first = first + jnp.where(grp > s, cnt[s], 0)
        last = last + jnp.where(grp >= s, cnt[s], 0)
    isub = lax.broadcasted_iota(jnp.int32, (BLK, SHARDS * BLK), 0)
    for lv in range(CHIPS):
        num = mod + (lv * ROWS + j * BLK)
        sel = jnp.where((first <= num) & (num < last), mod, -1)
        unp[lv * BLK:(lv + 1) * BLK, :] = jnp.where(isub == sel, 1.0, 0.0).astype(BF)

    own_kv.wait()

    def wait_kv(i, _):
        d = (c + SHARDS - i) % SHARDS
        remote(skv.at[0, pl.ds(0, BLK)], rkv.at[pl.ds(pl.multiple_of(d * BLK, BLK), BLK)],
               kv_s.at[d], kv_r.at[d], (d, t)).wait_recv()
        return 0
    lax.fori_loop(1, SHARDS, wait_kv, 0)
    mine = jnp.dot(unp[...], rkv[...], preferred_element_type=F32).astype(BF)
    for lv in range(CHIPS):
        kv[core, lv, j] = mine[lv * BLK:(lv + 1) * BLK]

    def block(b):
        return kv.at[core, :, b]

    def ring(b, way):
        dev = [(ctx_of(xl, (z + 1) % 8, core), t), (ctx_of(xl, (z + 7) % 8, core), t),
               (ctx_of(1 - xl, z, core), t), (c + 1 - 2 * core, t)][way]
        rsem = die_r.at[b] if way == 3 else ring_r.at[b]
        return remote(block(b), block(b), ring_s.at[way, b], rsem, dev)
    started = []

    def go(b, way):
        cp = ring(b, way)
        cp.start()
        started.append(cp)

    def arrive(b):
        remote(block(b), block(b), ring_s.at[0, b], ring_r.at[b], (c, t)).wait_recv()

    for way in (2, 0, 1, 3):
        go(j, way)
    jx = (1 - xl) * 8 + z
    arrive(jx)
    for way in (0, 1, 3):
        go(jx, way)
    for d in range(1, 5):
        zl, zr = (z + 8 - d) % 8, (z + d) % 8
        for col, rmax, lmax in ((xl, 4, 3), (1 - xl, 3, 4)):
            if d <= rmax:
                b = col * 8 + zl
                arrive(b)
                if d < rmax:
                    go(b, 0)
                go(b, 3)
            if d <= lmax:
                b = col * 8 + zr
                arrive(b)
                if d < lmax:
                    go(b, 1)
                go(b, 3)
        if d == 1:
            own_q.wait()

            def wait_q(i, _):
                e = (c + SHARDS - i) % SHARDS
                remote(sq.at[0, pl.ds(0, BLK)], rq.at[pl.ds(pl.multiple_of(e * BLK, BLK), BLK)],
                       q_s.at[e], q_r.at[e], (e, t)).wait_recv()
                return 0
            lax.fori_loop(1, SHARDS, wait_q, 0)
            qo[...] = jnp.dot(unp[...], rq[...], preferred_element_type=F32).astype(BF)

    w_own.wait()

    def half_rows(b, cr):
        return wf.at[pl.ds(pl.multiple_of(b * 512 + cr * half, half), half)]
    passed = []
    for n in range(7):
        b = w_peers[n][1]
        remote(half_rows(b, core), half_rows(b, core), w_s.at[n], w_r.at[b], (c, t)).wait_recv()
        cp = remote(half_rows(b, core), half_rows(b, core), wd_s.at[n], wd_r.at[b],
                    (c + 1 - 2 * core, t))
        cp.start()
        passed.append(cp)
    for n in range(7):
        b = w_peers[n][1]
        remote(half_rows(b, core), half_rows(b, 1 - core), wd_s.at[n], wd_r.at[b],
               (c, t)).wait_recv()
    for cp in passed:
        cp.wait_send()
    for n in range(7):
        w_copy(n).wait_send()
    for cp in started:
        cp.wait_send()

    def wait_die(b, _):
        ref = kv.at[1 - core, :, b]
        remote(ref, ref, ring_s.at[3, b], die_r.at[b], (c, t)).wait_recv()
        return 0
    lax.fori_loop(0, CHIPS, wait_die, 0)

    def wait_sends(i, _):
        d = (c + i) % SHARDS
        kv_copy(d).wait_send()
        q_copy(d).wait_send()
        return 0
    lax.fori_loop(1, SHARDS, wait_sends, 0)


def exchange(cnt, rank, q, k, v, w):
    dma = pltpu.SemaphoreType.DMA
    consts = [jnp.asarray(a) for a in tables()]
    vm = pl.BlockSpec(memory_space=VMEM)
    return pl.pallas_call(
        exchange_kernel,
        out_shape=[jax.ShapeDtypeStruct((ROWS, 2 * HD), BF),
                   jax.ShapeDtypeStruct((2, CHIPS, CHIPS, BLK, HD), BF),
                   jax.ShapeDtypeStruct((4096, 1024), BF)],
        in_specs=[pl.BlockSpec(memory_space=pltpu.SMEM)] + [vm] * 9 + [pl.BlockSpec(memory_space=pl.ANY)],
        out_specs=[vm, vm, pl.BlockSpec(memory_space=pl.ANY)],
        scratch_shapes=[
            VMEM((ROWS, 6 * HD), BF), VMEM((2, ROWS, 2 * HD), BF), VMEM((2, ROWS, HD), BF),
            VMEM((SHARDS * BLK, 2 * HD), BF), VMEM((SHARDS * BLK, HD), BF), VMEM((ROWS, SHARDS * BLK), BF),
            dma((SHARDS,)), dma((SHARDS,)), dma((SHARDS,)), dma((SHARDS,)),
            dma((4, CHIPS)), dma((CHIPS,)), dma((CHIPS,)),
            dma((8,)), dma((8,)), dma((8,)), dma((8,)), dma((3,)),
        ],
        compiler_params=pltpu.CompilerParams(
            collective_id=0, has_side_effects=True, vmem_limit_bytes=48 << 20),
        name="exchange",
    )(cnt, rank, q, k, v, *consts, w)


QL = 4
KC = 768


def attend_kernel(q, kv, o, qs):
    j = lax.axis_index("ctx") // 2
    tok = QL * BLK
    rows = 2 * tok
    for b in range(CHIPS // QL):
        qs[:tok] = q[b * tok:(b + 1) * tok, :HD]
        qs[tok:] = q[b * tok:(b + 1) * tok, HD:]
        qv = qs[...]

        def step(kc, state, masked):
            m, l, acc = state
            at = pl.ds(pl.multiple_of(kc * KC, KC), KC)
            s = lax.dot_general(qv, kv[0, at, :], (((1,), (1,)), ((), ())), preferred_element_type=F32)
            if masked is not None:
                r = lax.broadcasted_iota(jnp.int32, (rows, KC), 0)
                r = jnp.where(r >= tok, r - tok, r)
                lim = jnp.full((rows, KC), -1, jnp.int32)
                lim = jnp.where(r >= (masked + 1) * BLK, KC, lim)
                inside = (r >= masked * BLK) & (r < (masked + 1) * BLK)
                lim = jnp.where(inside, r - masked * BLK + j * BLK, lim)
                col = lax.broadcasted_iota(jnp.int32, (rows, KC), 1)
                s = jnp.where(col <= lim, s, -1e30)
            mn = jnp.maximum(m, jnp.max(s, axis=1, keepdims=True))
            a = jnp.exp2(m - mn)
            p = jnp.exp2(s - mn)
            l = l * a + jnp.sum(p, axis=1, keepdims=True)
            acc = acc * a + jnp.dot(p.astype(BF), kv[1, at, :], preferred_element_type=F32)
            return mn, l, acc

        state = (jnp.full((rows, 1), -1e30, F32), jnp.zeros((rows, 1), F32), jnp.zeros((rows, HD), F32))
        if b > 0:
            state = lax.fori_loop(0, b * QL, lambda kc, st: step(kc, st, None), state)
        for lv in range(QL):
            state = step(b * QL + lv, state, lv)
        m, l, acc = state
        out = (acc / l).astype(BF)
        o[b * tok:(b + 1) * tok, :HD] = out[:tok]
        o[b * tok:(b + 1) * tok, HD:] = out[tok:]


def attend(q, kv):
    vm = pl.BlockSpec(memory_space=VMEM)
    return pl.pallas_call(
        attend_kernel,
        out_shape=jax.ShapeDtypeStruct((ROWS, 2 * HD), BF),
        in_specs=[vm, vm],
        out_specs=vm,
        scratch_shapes=[VMEM((2 * QL * BLK, HD), BF)],
        compiler_params=pltpu.CompilerParams(vmem_limit_bytes=48 << 20),
        name="attend",
    )(q, kv)


def project_kernel(att, w, out, af, wv, acc, a_s, a_r, g_s, g_r, loc):
    me = place()
    c, t, core, z, xl, j, y, xh = (me[n] for n in ("c", "t", "core", "z", "xl", "j", "y", "xh"))
    bar = pltpu.get_barrier_semaphore()
    load = pltpu.make_async_copy(w, wv, loc.at[0])
    load.start()

    def target(lv):
        return 2 * lv + xl

    def source(n):
        return ctx_of(core, n // 2, n % 2)

    for lv in range(CHIPS):
        pl.semaphore_signal(bar, inc=1, device_id=(target(lv), t), device_id_type=MESH)
    for n in range(CHIPS):
        pl.semaphore_signal(bar, inc=1, device_id=(source(n), t), device_id_type=MESH)
    gat = [(c, y * 2 + 1 - xh), (c, ((y + 1) % 4) * 2 + xh), (c, ((y + 3) % 4) * 2 + xh)]
    for dev in gat:
        pl.semaphore_signal(bar, inc=1, device_id=dev, device_id_type=MESH)
    pl.semaphore_wait(bar, 2 * CHIPS + 3)

    slot = z * 2 + core
    here = (pl.ds(pl.multiple_of((j % 8) * BLK, BLK), BLK), pl.ds(pl.multiple_of(core * 256, 256), 256))

    def place_copy(lv):
        return remote(att.at[pl.ds(lv * BLK, BLK)], af.at[(t,) + here], a_s.at[lv], a_r.at[slot],
                      (target(lv), t))

    def own_copy(lv):
        return pltpu.make_async_copy(att.at[pl.ds(lv * BLK, BLK)], af.at[(t,) + here], loc.at[1])

    for lv in range(CHIPS):
        @pl.when(target(lv) != c)
        def _():
            place_copy(lv).start()

        @pl.when(target(lv) == c)
        def _():
            own_copy(lv).start()
    for n in range(CHIPS):
        rows = pl.ds((n // 2) * BLK, BLK)
        cs = pl.ds((n % 2) * 256, 256)

        @pl.when(source(n) != c)
        def _():
            remote(att.at[pl.ds(0, BLK)], af.at[t, rows, cs], a_s.at[n], a_r.at[n], (c, t)).wait_recv()

        @pl.when(source(n) == c)
        def _():
            own_copy(0).wait()

    sent = []

    def go(b, way):
        cp = remote(af.at[b], af.at[b], g_s.at[way, b], g_r.at[b], gat[way])
        cp.start()
        sent.append(cp)

    def arrive(b):
        remote(af.at[b], af.at[b], g_s.at[0, b], g_r.at[b], (c, t)).wait_recv()

    def mul(b, first=False):
        rows = pl.ds(pl.multiple_of(b * 512, 512), 512)

        @pl.loop(0, 4)
        def _(n):
            cs = pl.ds(pl.multiple_of(n * 256, 256), 256)
            part = jnp.dot(af[b], wv[rows, cs], preferred_element_type=F32)
            acc[:, cs] = part if first else acc[:, cs] + part

    for way in (0, 1, 2):
        go(t, way)
    load.wait()
    mul(t, True)
    bx = y * 2 + 1 - xh
    arrive(bx)
    go(bx, 1)
    go(bx, 2)
    mul(bx)
    lo, hi, opp = (y + 3) % 4, (y + 1) % 4, (y + 2) % 4
    arrive(lo * 2 + xh)
    go(lo * 2 + xh, 1)
    mul(lo * 2 + xh)
    arrive(hi * 2 + xh)
    mul(hi * 2 + xh)
    arrive(hi * 2 + 1 - xh)
    go(hi * 2 + 1 - xh, 2)
    mul(hi * 2 + 1 - xh)
    arrive(lo * 2 + 1 - xh)
    mul(lo * 2 + 1 - xh)
    arrive(opp * 2 + xh)
    mul(opp * 2 + xh)
    arrive(opp * 2 + 1 - xh)
    mul(opp * 2 + 1 - xh)
    out[...] = acc[...].astype(BF)
    for cp in sent:
        cp.wait_send()
    for lv in range(CHIPS):
        @pl.when(target(lv) != c)
        def _():
            place_copy(lv).wait_send()


def project(att, w):
    dma = pltpu.SemaphoreType.DMA
    vm = pl.BlockSpec(memory_space=VMEM)
    return pl.pallas_call(
        project_kernel,
        out_shape=jax.ShapeDtypeStruct((384, 1024), BF),
        in_specs=[vm, pl.BlockSpec(memory_space=pl.ANY)],
        out_specs=vm,
        scratch_shapes=[
            VMEM((8, 384, 512), BF), VMEM((4096, 1024), BF), VMEM((384, 1024), F32),
            dma((CHIPS,)), dma((CHIPS,)), dma((3, 8)), dma((8,)), dma((2,)),
        ],
        compiler_params=pltpu.CompilerParams(
            collective_id=1, has_side_effects=True, vmem_limit_bytes=48 << 20),
        name="project",
    )(att, w)


def local(query, key, value, keep_rank, kept_count, out_weight):
    q, kv, w = exchange(kept_count, keep_rank, query, key, value, out_weight)
    att = attend(q, kv.reshape(2, KEPT, HD))
    return project(att, w)


def solution(mesh):
    placed = (P("ctx", "tp"), P("ctx", "tp"), P("ctx", "tp"), P("ctx", None), P(), P("tp", None))
    return jax.shard_map(
        local, mesh=mesh, in_specs=placed, out_specs=P("ctx", "tp"), check_vma=False)
```

time: 555 us -> 169 us (0.30)
  waiting for transfers between devices: 215 us -> 0 us
  Pallas kernels: 0 us -> 159 us
  matrix products: 129 us -> 0 us
  local copies, waits for them, and re-layouts: 70 us -> 9.43 us
  other arithmetic: 56.3 us -> 0 us
  blocking collectives: 49.5 us -> 0 us
  starting transfers between devices: 16.8 us -> 0 us
  between operations: 13.4 us -> 0.03 us
    pallas_call x0 -> x3, Pallas kernels: none -> 159 us  [the longest x1 81.6 us: exchange(): pl.pallas_call(exchange_kernel, out_shape=[jax.ShapeDtypeStruct((ROWS, 2...]
    dot_general x49 -> x0, matrix products: 129 us -> none  [the longest x24 77.7 us: absorb_block(): jnp.einsum('kgrp,pkd->kgrd', weights_b, value_heads, preferred_element_ty...]
    reduce_scatter x1 -> x0, waiting for transfers between devices: 102 us -> none  [local(): lax.psum_scatter(lax.dot_general(out_weight, attention, (((0,), (1,)), ((...]
    all_gather x2 -> x0, waiting for transfers between devices: 77 us -> none  [the longest x1 67.6 us: local(): key_piece = lax.all_gather(key_local, 'ctx', axis=0, tiled=True)]
    all_to_all x2 -> x0, blocking collectives: 49.5 us -> none  [the longest x1 34.7 us: local(): lax.all_to_all(projected, 'ctx', split_axis=0, concat_axis=0, tiled=True)]
    all_to_all x2 -> x0, waiting for transfers between devices: 35.9 us -> none  [the longest x1 26 us: local(): lax.all_to_all(pack_rows(rot_query), 'ctx', split_axis=0, concat_axis=0,...]
    dynamic_slice x24 -> x0, local copies, waits for them, and re-layouts: 30.4 us -> none  [local(): lax.scan(one_turn, state, (key_blocks, value_blocks, block_firsts))]
    reduce_sum x27 -> x0, other arithmetic: 20.3 us -> none  [the longest x24 18.8 us: absorb_block(): new_sum = run_sum * rescale + jnp.sum(weights, axis=-1)]
  transfers between devices with their start and end apart: 5 -> 0, of which waited for: 5 -> 0; matrix products, arithmetic and copies ran while one was open for 3% -> 0% of each run, Pallas kernels for 0% -> 0%
where the time goes in v1:
time: 169 us; the launch traced here: 168 us
  Pallas kernels  159 us (94%)
  local copies, waits for them, and re-layouts  9.43 us (6%)
    pallas_call x1, Pallas kernels, exchange(): pl.pallas_call(exchange_kernel, out_shape=[jax.ShapeDtypeStruct((ROWS, 2...  81.6 us
    pallas_call x1, Pallas kernels, project(): pl.pallas_call(project_kernel, out_shape=jax.ShapeDtypeStruct((384, 1024)...  46.6 us
    pallas_call x1, Pallas kernels, attend(): pl.pallas_call(attend_kernel, out_shape=jax.ShapeDtypeStruct((ROWS, 2 * H...  30.6 us
    unnamed x21, local copies, waits for them, and re-layouts  9.43 us

profile of v1, /device:TPU:1, one launch (start us, length us, event | category | flops | bytes accessed | tf_op | source)
XLA Modules:
  0.0 168.3 jit_solution(5407833038225046641)
XLA Ops:
  0.0 0.0 copy-start
  0.0 1.1 copy-done
  1.1 0.0 copy-start.1
  1.1 1.0 copy-done.1
  2.1 0.0 copy-start.2
  2.1 1.0 copy-done.2
  3.1 0.0 copy-start.3
  3.1 0.9 copy-done.3
  4.1 0.0 copy-start.4
  4.1 0.9 copy-done.4
  5.0 0.0 copy-start.5
  5.0 0.8 copy-done.5
  5.8 0.0 copy-start.6
  5.8 0.7 copy-done.6
  6.5 0.0 copy-start.7
  6.5 0.7 copy-done.7
  7.2 0.0 copy-start.8
  7.2 0.7 copy-done.8
  7.9 0.0 copy-start.9
  7.9 0.7 copy-done.9
  8.6 81.6 %exchange.1 = (bf16[768,256]{1,0:T(8,128)(2,1)S(1)}, bf16[2,16,16,48,128]{4,3,2,1,0:T(8,128)(2,1)}, bf16[4096,1024]{1,0:T(8,128)(2,1)}) custom-call(s32[32]{0:T(128)S(1)} %copy-done.9, s32[1,768]{1,0:T(1,128)S(1)} %copy-done.8, bf16[768,512]{1,0:T(8,128)(2,1)S(1)} %copy-done, bf16[768,128]{1,0:T(8,128)(2,1)S(1)} %copy-done.3, ...), custom_call_target="tpu_custom_call" | custom-call | tf_op jit(solution)/shard_map/exchange/pallas_call | solution.py:265
  90.1 30.6 %attend.1.att = bf16[768,256]{1,0:T(8,128)(2,1)S(1)} custom-call(bf16[768,256]{1,0:T(8,128)(2,1)S(1)} %get-tuple-element.8.q, bf16[2,12288,128]{2,1,0:T(8,128)(2,1)} %bitcast.1), custom_call_target="tpu_custom_call" | custom-call | tf_op jit(solution)/shard_map/attend/pallas_call | solution.py:331
  120.7 46.6 %project.1 = bf16[384,1024]{1,0:T(8,128)(2,1)S(1)} custom-call(bf16[768,256]{1,0:T(8,128)(2,1)S(1)} %attend.1.att, bf16[4096,1024]{1,0:T(8,128)(2,1)} %get-tuple-element.10.w), custom_call_target="tpu_custom_call" | custom-call | tf_op jit(solution)/shard_map/project/pallas_call | solution.py:449
  167.4 0.9 copy.13
Async XLA Ops:
  0.0 1.1 copy-start
  1.1 1.0 copy-start.1
  2.1 1.0 copy-start.2
  3.1 0.9 copy-start.3
  4.1 0.9 copy-start.4
  5.0 0.8 copy-start.5
  5.8 0.7 copy-start.6
  6.5 0.7 copy-start.7
  7.2 0.7 copy-start.8
  7.9 0.7 copy-start.9

commit v2 on v0

v2 whole, which is shorter than its diff:
```python
import math

import jax
import jax.numpy as jnp
import numpy as np
from jax import lax
from jax.experimental import pallas as pl
from jax.experimental.pallas import tpu as pltpu
from jax.sharding import PartitionSpec as P

HD = 128
ROWS = 768
BLK = 48
CHIPS = 16
SHARDS = 32
SLOTS = SHARDS * BLK
QL = 4
GROUPS = CHIPS // QL
LROWS = 2 * BLK
QROWS = QL * LROWS
KC = 3072
OUT = 1024
NT = (((1,), (1,)), ((), ()))
MESH = pl.DeviceIdType.MESH
VMEM = pltpu.VMEM
BF = jnp.bfloat16
F32 = jnp.float32


def tables():
    freq = 1000000.0 ** (-(np.arange(HD // 2) * 2.0 / HD))
    sign = np.concatenate([-np.ones(HD // 2), np.ones(HD // 2)])
    both = np.concatenate([freq, freq])
    own = np.arange(ROWS)[:, None] * both
    base = (np.arange(SHARDS) * ROWS)[:, None] * both
    col = np.arange(SLOTS)
    cols = np.zeros((8, SLOTS), np.int32)
    cols[0], cols[1] = col // BLK, col % BLK
    f = lambda a, b: np.stack([np.cos(a), np.sin(b) * sign]).astype(np.float32)
    return f(own, own), f(base, base), cols


def ctx_of(xl, z, core):
    return xl * 16 + z * 2 + core


def remote(src, dst, ssem, rsem, dev):
    return pltpu.make_async_remote_copy(
        src_ref=src, dst_ref=dst, send_sem=ssem, recv_sem=rsem, device_id=dev, device_id_type=MESH)


def at16(first, size):
    return pl.ds(pl.multiple_of(first, 16), size)


def layer_kernel(cnt, rank_h, q_h, k_h, v_h, own_h, base_h, cols_h, w_h, out,
                 rank, qin, kin, vin, own, base, cols,
                 xs, sq, skv, rq, rkv, unp, qs, kv, m_s, acc_s, o_s, af, wf, po,
                 ld, kv_s, kv_r, q_s, q_r, ring_s, ring_r, die_r, w_s, w_r, wd_s, wd_r,
                 a_s, a_r, g_s, g_r):
    c, t = lax.axis_index("ctx"), lax.axis_index("tp")
    core, z, xl, j, y, xh = c % 2, (c // 2) % 8, c // 16, c // 2, t // 2, t % 2
    mate = c + 1 - 2 * core
    bar = pltpu.get_barrier_semaphore()

    loads = {}
    wcol = pl.ds(pl.multiple_of(t * OUT, OUT), OUT)
    for n, (name, src, dst) in enumerate([
            ("rank", rank_h, rank), ("k", k_h, kin), ("own", own_h, own), ("base", base_h, base),
            ("v", v_h, vin), ("q", q_h, qin), ("cols", cols_h, cols),
            ("w", w_h.at[:, wcol], wf.at[pl.ds(pl.multiple_of(t * 512, 512), 512)])]):
        loads[name] = pltpu.make_async_copy(src, dst, ld.at[n])
        loads[name].start()

    def hail(i, _):
        pl.semaphore_signal(bar, inc=1, device_id=((c + i) % SHARDS, t), device_id_type=MESH)
        return 0
    lax.fori_loop(1, SHARDS, hail, 0)
    cx = ctx_of(1 - xl, z, core)
    w_peers = [(c, ((y + d) % 4) * 2 + xh) for d in (1, 2, 3)]
    w_peers += [(cx, ((y + d) % 4) * 2 + (1 - xh)) for d in (0, 1, 2, 3)]
    gat = [(c, y * 2 + 1 - xh), (c, ((y + 1) % 4) * 2 + xh), (c, ((y + 3) % 4) * 2 + xh)]
    for peer in w_peers + gat[:1]:
        pl.semaphore_signal(bar, inc=1, device_id=peer, device_id_type=MESH)

    loads["rank"].wait()
    my_count = cnt[c]
    start = jnp.int32(0)
    for s in range(SHARDS):
        start = start + jnp.where(s < c, cnt[s], 0)
    kept = rank[...] < my_count
    keptf = jnp.where(kept, 1.0, 0.0).astype(BF)
    i0 = lax.broadcasted_iota(jnp.int32, (ROWS, ROWS), 0)
    i1 = lax.broadcasted_iota(jnp.int32, (ROWS, ROWS), 1)
    tri = jnp.where(i0 < i1, 1.0, 0.0).astype(BF)
    order = jnp.dot(jnp.broadcast_to(keptf, (16, ROWS)), tri, preferred_element_type=F32)[0:1]
    slot = order.astype(jnp.int32) + lax.rem(start, jnp.int32(ROWS))
    slot = jnp.where(slot >= ROWS, slot - ROWS, slot)
    slot = jnp.where(kept, slot, -1)
    perm = jnp.where(i0 == slot, 1.0, 0.0).astype(BF)

    for name in ("own", "base", "k", "v"):
        loads[name].wait()
    cbr, sbr = base[0, pl.ds(c, 1), :], base[1, pl.ds(c, 1), :]
    civ, siv = own[0], own[1]
    cosv = civ * cbr - siv * sbr
    sinv = siv * cbr + civ * sbr

    def rotate(x, scale):
        x = x.astype(F32)
        r = x * cosv + pltpu.roll(x, HD // 2, 1) * sinv
        return (r * scale if scale else r).astype(BF)
    xs[:, 4 * HD:5 * HD] = rotate(kin[...], None)
    xs[:, 5 * HD:] = vin[...]
    kvp = jnp.dot(perm, xs[:, 4 * HD:], preferred_element_type=F32).astype(BF)
    skv[0] = kvp[:, :HD]
    skv[1] = kvp[:, HD:]
    pl.semaphore_wait(bar, SHARDS - 1 + 8)

    def kv_copy(d):
        return remote(skv.at[d % 2, at16((d // 2) * BLK, BLK)], rkv.at[at16(c * BLK, BLK)],
                      kv_s.at[d], kv_r.at[c], (d, t))

    def q_copy(d):
        return remote(sq.at[d % 2, at16((d // 2) * BLK, BLK)], rq.at[at16(c * BLK, BLK)],
                      q_s.at[d], q_r.at[c], (d, t))

    def start_kv(i, _):
        kv_copy((c + i) % SHARDS).start()
        return 0
    lax.fori_loop(1, SHARDS, start_kv, 0)
    own_kv = pltpu.make_async_copy(skv.at[core, at16(j * BLK, BLK)], rkv.at[at16(c * BLK, BLK)], ld.at[8])
    own_kv.start()

    half = 256

    def half_rows(b, cr):
        return wf.at[pl.ds(pl.multiple_of(b * 512 + cr * half, half), half)]

    def w_copy(n):
        peer = w_peers[n]
        return remote(w_h.at[pl.ds(pl.multiple_of(core * half, half), half),
                             pl.ds(pl.multiple_of(peer[1] * OUT, OUT), OUT)],
                      half_rows(t, core), w_s.at[n], w_r.at[t], peer)
    for n in range(7):
        w_copy(n).start()

    scale = math.log2(math.e) / math.sqrt(HD)
    loads["q"].wait()
    for h in range(4):
        xs[:, h * HD:(h + 1) * HD] = rotate(qin[:, h * HD:(h + 1) * HD], scale)
    qp = jnp.dot(perm, xs[:, :4 * HD], preferred_element_type=F32).astype(BF)
    sq[0] = qp[:, :2 * HD]
    sq[1] = qp[:, 2 * HD:]

    def start_q(i, _):
        q_copy((c + i) % SHARDS).start()
        return 0
    lax.fori_loop(1, SHARDS, start_q, 0)
    own_q = pltpu.make_async_copy(sq.at[core, at16(j * BLK, BLK)], rq.at[at16(c * BLK, BLK)], ld.at[9])
    own_q.start()

    loads["cols"].wait()
    grp, mod = cols[0:1, :], cols[1:2, :]
    first = jnp.zeros((1, SLOTS), jnp.int32)
    last = jnp.zeros((1, SLOTS), jnp.int32)
    for s in range(SHARDS):
        first = first + jnp.where(grp > s, cnt[s], 0)
        last = last + jnp.where(grp >= s, cnt[s], 0)
    isub = lax.broadcasted_iota(jnp.int32, (BLK, SLOTS), 0)
    for lv in range(CHIPS):
        num = mod + (lv * ROWS + j * BLK)
        sel = jnp.where((first <= num) & (num < last), mod, -1)
        unp[lv * BLK:(lv + 1) * BLK, :] = jnp.where(isub == sel, 1.0, 0.0).astype(BF)
    m_s[...] = jnp.full(m_s.shape, -1e30, F32)
    acc_s[...] = jnp.zeros(acc_s.shape, F32)

    own_kv.wait()

    def wait_kv(i, _):
        d = (c + SHARDS - i) % SHARDS
        remote(skv.at[0, pl.ds(0, BLK)], rkv.at[at16(d * BLK, BLK)], kv_s.at[d], kv_r.at[d],
               (d, t)).wait_recv()
        return 0
    lax.fori_loop(1, SHARDS, wait_kv, 0)
    mine = jnp.dot(unp[...], rkv[...], preferred_element_type=F32).astype(BF)
    for lv in range(CHIPS):
        kv[core, lv, j] = mine[lv * BLK:(lv + 1) * BLK]

    sent = []
    ways = [(ctx_of(xl, (z + 1) % 8, core), t), (ctx_of(xl, (z + 7) % 8, core), t), (cx, t), (mate, t)]
    RIGHT, LEFT, CROSS, DIE = range(4)

    def piece(g, b):
        return kv.at[core, pl.ds(g * QL, QL), b]

    def go(g, b, *to):
        for way in to:
            rsem = die_r.at[g, b] if way == DIE else ring_r.at[g, b]
            cp = remote(piece(g, b), piece(g, b), ring_s.at[way, g, b], rsem, ways[way])
            cp.start()
            sent.append(cp)

    def arrive(g, b, *to):
        remote(piece(g, b), piece(g, b), ring_s.at[0, g, b], ring_r.at[g, b], (mate, t)).wait_recv()
        go(g, b, *to)

    def same(d):
        return xl * 8 + (z + 8 + d) % 8

    def other(d):
        return (1 - xl) * 8 + (z + 8 + d) % 8

    def tick(g, k):
        if k == 0:
            go(g, j, RIGHT, LEFT, CROSS, DIE)
        elif k == 1:
            arrive(g, other(0), RIGHT, LEFT, DIE)
            arrive(g, same(-1), RIGHT, DIE)
            arrive(g, same(1), LEFT, DIE)
        elif k == 2:
            arrive(g, other(-1), RIGHT, DIE)
            arrive(g, other(1), DIE)
            arrive(g, same(-2), RIGHT, DIE)
            arrive(g, same(2), LEFT, CROSS, DIE)
        elif k == 3:
            arrive(g, other(-2), DIE)
            arrive(g, same(-3), CROSS, DIE)
            arrive(g, same(3), LEFT, CROSS, DIE)
            arrive(g, other(2), DIE)
        else:
            arrive(g, same(4), CROSS, DIE)
            arrive(g, other(-3), DIE)
            arrive(g, other(3), DIE)
            arrive(g, other(4), DIE)

    def whole(g):
        def wait_die(b, _):
            ref = kv.at[1 - core, pl.ds(g * QL, QL), b]
            remote(ref, ref, ring_s.at[0, g, b], die_r.at[g, b], (mate, t)).wait_recv()
            return 0
        lax.fori_loop(0, CHIPS, wait_die, 0)

    def update(r0, n, s, vals):
        rows = pl.ds(r0, n)
        mo = m_s[rows, :]
        mn = jnp.maximum(mo, jnp.max(s, axis=1, keepdims=True))
        a = jnp.exp2(mo - mn)
        p = jnp.exp2(s - jnp.tile(mn, (1, s.shape[1] // HD))).astype(BF)
        m_s[rows, :] = mn
        vo = jnp.concatenate([vals, jnp.ones(vals.shape, BF)], axis=1)
        acc_s[rows, :] = acc_s[rows, :] * jnp.tile(a, (1, 2)) + jnp.dot(p, vo, preferred_element_type=F32)

    def unit(g, b):
        r0 = b * QROWS
        if b > g:
            n = QROWS // 2

            @pl.loop(0, QL * ROWS // KC)
            def _(i):
                lv = pl.ds(g * QL + i * (KC // ROWS), KC // ROWS)
                kk = kv[0, lv].reshape(KC, HD)
                vv = kv[1, lv].reshape(KC, HD)
                ss = [lax.dot_general(qs[r0 + h * n:r0 + (h + 1) * n, :], kk, NT, preferred_element_type=F32)
                      for h in range(2)]
                for h in range(2):
                    update(r0 + h * n, n, ss[h], vv)
            return
        for i in range(QL):
            lv = g * QL + i
            rs, n = r0 + i * LROWS, QROWS - i * LROWS
            kk = kv[0, lv].reshape(ROWS, HD)
            vv = kv[1, lv].reshape(ROWS, HD)
            s = lax.dot_general(qs[rs:rs + n, :], kk, NT, preferred_element_type=F32)
            r = lax.broadcasted_iota(jnp.int32, (LROWS, ROWS), 0)
            lim = jnp.where(r >= BLK, r - BLK, r) + j * BLK
            col = lax.broadcasted_iota(jnp.int32, (LROWS, ROWS), 1)
            top = jnp.where(col <= lim, s[:LROWS], -1e30)
            s = top if n == LROWS else jnp.concatenate([top, s[LROWS:]], axis=0)
            update(rs, n, s, vv)

    slot_a = z * 2 + core

    def here(h):
        return af.at[t, at16(z * BLK, BLK), pl.ds(pl.multiple_of(core * 256 + h * HD, HD), HD)]

    def o_copy(lv, h):
        return remote(o_s.at[pl.ds(lv * LROWS + h * BLK, BLK)], here(h), a_s.at[lv, h], a_r.at[slot_a, h],
                      (2 * lv + xl, t))

    def o_own(lv, h):
        return pltpu.make_async_copy(o_s.at[pl.ds(lv * LROWS + h * BLK, BLK)], here(h), ld.at[10 + h])

    def finish(b):
        rows = pl.ds(b * QROWS, QROWS)
        o_s[rows, :] = (acc_s[rows, :HD] / acc_s[rows, HD:]).astype(BF)
        for lv in range(b * QL, (b + 1) * QL):
            @pl.when(2 * lv + xl != c)
            def _():
                o_copy(lv, 0).start()
                o_copy(lv, 1).start()

            @pl.when(2 * lv + xl == c)
            def _():
                o_own(lv, 0).start()
                o_own(lv, 1).start()

    def take_queries():
        own_q.wait()

        def wait_q(i, _):
            e = (c + SHARDS - i) % SHARDS
            remote(sq.at[0, pl.ds(0, BLK)], rq.at[at16(e * BLK, BLK)], q_s.at[e], q_r.at[e],
                   (e, t)).wait_recv()
            return 0
        lax.fori_loop(1, SHARDS, wait_q, 0)
        r = jnp.dot(unp[...], rq[...], preferred_element_type=F32).astype(BF)
        for lv in range(CHIPS):
            for h in range(2):
                qs[lv * LROWS + h * BLK:lv * LROWS + (h + 1) * BLK, :] = r[
                    lv * BLK:(lv + 1) * BLK, h * HD:(h + 1) * HD]

    work = {g: [(g, b) for b in range(g, GROUPS)] for g in range(GROUPS)}
    ready, todo = 0, []
    for step in range(3 * (GROUPS - 1) + 5):
        for g in range(GROUPS):
            if 0 <= step - 3 * g <= 4:
                tick(g, step - 3 * g)
        if step == 4:
            take_queries()
        if step - 3 * ready == 4:
            whole(ready)
            todo += work[ready]
            ready += 1
        for _ in range(1 if ready < GROUPS else len(todo)):
            if todo:
                g, b = todo.pop(0)
                unit(g, b)
                if g == b:
                    finish(b)

    passed = []
    for n in range(7):
        b = w_peers[n][1]
        remote(half_rows(b, core), half_rows(b, core), w_s.at[n], w_r.at[b], (mate, t)).wait_recv()
        cp = remote(half_rows(b, core), half_rows(b, core), wd_s.at[n], wd_r.at[b], (mate, t))
        cp.start()
        passed.append(cp)
    loads["w"].wait()

    for n in range(CHIPS):
        src = ctx_of(core, n // 2, n % 2)
        for h in range(2):
            ref = af.at[t, pl.ds((n // 2) * BLK, BLK), pl.ds((n % 2) * 256 + h * HD, HD)]

            @pl.when(src != c)
            def _():
                remote(o_s.at[pl.ds(0, BLK)], ref, a_s.at[n, h], a_r.at[n, h], (mate, t)).wait_recv()

            @pl.when(src == c)
            def _():
                o_own(0, h).wait()

    def pass_on(b, *to):
        for way in to:
            cp = remote(af.at[b], af.at[b], g_s.at[way, b], g_r.at[b], gat[way])
            cp.start()
            sent.append(cp)

    def got(b, *to):
        remote(af.at[b], af.at[b], g_s.at[0, b], g_r.at[b], (mate, t)).wait_recv()
        pass_on(b, *to)

    def mul(b, begin=False):
        rows = pl.ds(pl.multiple_of(b * 512, 512), 512)
        if not begin:
            ref = half_rows(b, 1 - core)
            remote(ref, ref, wd_s.at[0], wd_r.at[b], (mate, t)).wait_recv()

        @pl.loop(0, OUT // 256)
        def _(n):
            cs = pl.ds(pl.multiple_of(n * 256, 256), 256)
            part = jnp.dot(af[b], wf[rows, cs], preferred_element_type=F32)
            po[:, cs] = part if begin else po[:, cs] + part

    lo, hi, opp = (y + 3) % 4, (y + 1) % 4, (y + 2) % 4
    pass_on(t, 0, 1, 2)
    mul(t, True)
    bx = y * 2 + 1 - xh
    got(bx, 1, 2)
    got(lo * 2 + xh, 1)
    mul(bx)
    mul(lo * 2 + xh)
    got(hi * 2 + xh)
    mul(hi * 2 + xh)
    got(hi * 2 + 1 - xh, 2)
    mul(hi * 2 + 1 - xh)
    got(lo * 2 + 1 - xh)
    mul(lo * 2 + 1 - xh)
    got(opp * 2 + xh)
    mul(opp * 2 + xh)
    got(opp * 2 + 1 - xh)
    mul(opp * 2 + 1 - xh)
    out[...] = po[...].astype(BF)

    for cp in passed + sent:
        cp.wait_send()
    for n in range(7):
        w_copy(n).wait_send()
    for lv in range(CHIPS):
        @pl.when(2 * lv + xl != c)
        def _():
            o_copy(lv, 0).wait_send()
            o_copy(lv, 1).wait_send()

    def wait_sends(i, _):
        d = (c + i) % SHARDS
        kv_copy(d).wait_send()
        q_copy(d).wait_send()
        return 0
    lax.fori_loop(1, SHARDS, wait_sends, 0)


def local(query, key, value, keep_rank, kept_count, out_weight):
    dma = pltpu.SemaphoreType.DMA
    consts = [jnp.asarray(a) for a in tables()]
    hbm = pl.BlockSpec(memory_space=pl.ANY)
    return pl.pallas_call(
        layer_kernel,
        out_shape=jax.ShapeDtypeStruct((384, OUT), BF),
        in_specs=[pl.BlockSpec(memory_space=pltpu.SMEM)] + [hbm] * 8,
        out_specs=pl.BlockSpec(memory_space=VMEM),
        scratch_shapes=[
            VMEM((1, ROWS), jnp.int32), VMEM((ROWS, 4 * HD), BF), VMEM((ROWS, HD), BF), VMEM((ROWS, HD), BF),
            VMEM((2, ROWS, HD), F32), VMEM((2, SHARDS, HD), F32), VMEM((8, SLOTS), jnp.int32),
            VMEM((ROWS, 6 * HD), BF), VMEM((2, ROWS, 2 * HD), BF), VMEM((2, ROWS, HD), BF),
            VMEM((SLOTS, 2 * HD), BF), VMEM((SLOTS, HD), BF), VMEM((ROWS, SLOTS), BF),
            VMEM((2 * ROWS, HD), BF), VMEM((2, CHIPS, CHIPS, BLK, HD), BF),
            VMEM((2 * ROWS, HD), F32), VMEM((2 * ROWS, 2 * HD), F32), VMEM((2 * ROWS, HD), BF),
            VMEM((8, 384, 512), BF), VMEM((4096, OUT), BF), VMEM((384, OUT), F32),
            dma((12,)), dma((SHARDS,)), dma((SHARDS,)), dma((SHARDS,)), dma((SHARDS,)),
            dma((4, GROUPS, CHIPS)), dma((GROUPS, CHIPS)), dma((GROUPS, CHIPS)),
            dma((8,)), dma((8,)), dma((8,)), dma((8,)),
            dma((CHIPS, 2)), dma((CHIPS, 2)), dma((3, 8)), dma((8,)),
        ],
        compiler_params=pltpu.CompilerParams(
            collective_id=0, has_side_effects=True, vmem_limit_bytes=56 << 20),
        cost_estimate=pl.CostEstimate(flops=13 * 10 ** 9, bytes_accessed=12 << 20, transcendentals=10 ** 7),
        name="layer",
    )(kept_count, keep_rank, query, key, value, *consts, out_weight)


def solution(mesh):
    placed = (P("ctx", "tp"), P("ctx", "tp"), P("ctx", "tp"), P("ctx", None), P(), P("tp", None))
    return jax.shard_map(
        local, mesh=mesh, in_specs=placed, out_specs=P("ctx", "tp"), check_vma=False)
```

time: 555 us -> 148 us (0.27)
  waiting for transfers between devices: 215 us -> 0 us
  Pallas kernels: 0 us -> 146 us
  matrix products: 129 us -> 0 us
  local copies, waits for them, and re-layouts: 70 us -> 2.06 us
  other arithmetic: 56.3 us -> 0 us
  blocking collectives: 49.5 us -> 0 us
  starting transfers between devices: 16.8 us -> 0 us
  between operations: 13.4 us -> 0.01 us
    pallas_call x0 -> x1, Pallas kernels: none -> 146 us  [local(): pl.pallas_call(layer_kernel, out_shape=jax.ShapeDtypeStruct((384, OUT), B...]
    dot_general x49 -> x0, matrix products: 129 us -> none  [the longest x24 77.7 us: absorb_block(): jnp.einsum('kgrp,pkd->kgrd', weights_b, value_heads, preferred_element_ty...]
    reduce_scatter x1 -> x0, waiting for transfers between devices: 102 us -> none  [local(): lax.psum_scatter(lax.dot_general(out_weight, attention, (((0,), (1,)), ((...]
    all_gather x2 -> x0, waiting for transfers between devices: 77 us -> none  [the longest x1 67.6 us: local(): key_piece = lax.all_gather(key_local, 'ctx', axis=0, tiled=True)]
    all_to_all x2 -> x0, blocking collectives: 49.5 us -> none  [the longest x1 34.7 us: local(): lax.all_to_all(projected, 'ctx', split_axis=0, concat_axis=0, tiled=True)]
    all_to_all x2 -> x0, waiting for transfers between devices: 35.9 us -> none  [the longest x1 26 us: local(): lax.all_to_all(pack_rows(rot_query), 'ctx', split_axis=0, concat_axis=0,...]
    dynamic_slice x24 -> x0, local copies, waits for them, and re-layouts: 30.4 us -> none  [local(): lax.scan(one_turn, state, (key_blocks, value_blocks, block_firsts))]
    reduce_sum x27 -> x0, other arithmetic: 20.3 us -> none  [the longest x24 18.8 us: absorb_block(): new_sum = run_sum * rescale + jnp.sum(weights, axis=-1)]
  transfers between devices with their start and end apart: 5 -> 0, of which waited for: 5 -> 0; matrix products, arithmetic and copies ran while one was open for 3% -> 0% of each run, Pallas kernels for 0% -> 0%
where the time goes in v2:
time: 148 us
  Pallas kernels  146 us (99%)
  local copies, waits for them, and re-layouts  2.06 us (1%)
    pallas_call x1, Pallas kernels, local(): pl.pallas_call(layer_kernel, out_shape=jax.ShapeDtypeStruct((384, OUT), B...  146 us

profile of v2, /device:TPU:1, one launch (start us, length us, event | category | flops | bytes accessed | tf_op | source)
XLA Modules:
  0.0 147.7 jit_solution(3582527108650421404)
XLA Ops:
  0.0 145.6 %layer.1 = bf16[384,1024]{1,0:T(8,128)(2,1)} custom-call(s32[32]{0:T(128)} %cnt.1, s32[1,768]{1,0:T(1,128)} %rank_h.1, bf16[768,512]{1,0:T(8,128)(2,1)} %q_h.1, bf16[768,128]{1,0:T(8,128)(2,1)} %k_h.1, bf16[768,128]{1,0:T(8,128)(2,1)} %v_h.1, f32[2,768,128]{2,1,0:T(8,128)} %constant.6.clone.own_h, f32[2,32,128]{2,1,0:T(8,128)} %constant.7.clone.base_h, ...), custom_call_target="tpu_custom_call" | custom-call | flops 12999999488 | bytes 12582912 | tf_op jit(solution)/shard_map/layer/pallas_call | solution.py:428
  145.7 2.1 %copy.11 = bf16[384,1024]{1,0:T(8,128)(2,1)} copy(bf16[384,1024]{1,0:T(8,128)(2,1)} %layer.1) | data formatting | bytes 1572864

commit v3 on v2

--- a/solution.py
+++ b/solution.py
@@ -18,7 +18,7 @@
 GROUPS = CHIPS // QL
 LROWS = 2 * BLK
 QROWS = QL * LROWS
-KC = 3072
+STAGGER = 1
 OUT = 1024
 NT = (((1,), (1,)), ((), ()))
 MESH = pl.DeviceIdType.MESH
@@ -62,6 +62,12 @@
     core, z, xl, j, y, xh = c % 2, (c // 2) % 8, c // 16, c // 2, t // 2, t % 2
     mate = c + 1 - 2 * core
     bar = pltpu.get_barrier_semaphore()
+
+    def landed(ref, sem):
+        remote(ref, ref, sem, sem, (mate, t)).wait_recv()
+
+    def left(ref, sem):
+        remote(ref, ref, sem, sem, (mate, t)).wait_send()
 
     loads = {}
     wcol = pl.ds(pl.multiple_of(t * OUT, OUT), OUT)
@@ -119,11 +125,11 @@
 
     def kv_copy(d):
         return remote(skv.at[d % 2, at16((d // 2) * BLK, BLK)], rkv.at[at16(c * BLK, BLK)],
-                      kv_s.at[d], kv_r.at[c], (d, t))
+                      kv_s.at[0], kv_r.at[0], (d, t))
 
     def q_copy(d):
         return remote(sq.at[d % 2, at16((d // 2) * BLK, BLK)], rq.at[at16(c * BLK, BLK)],
-                      q_s.at[d], q_r.at[c], (d, t))
+                      q_s.at[0], q_r.at[0], (d, t))
 
     def start_kv(i, _):
         kv_copy((c + i) % SHARDS).start()
@@ -141,7 +147,7 @@
         peer = w_peers[n]
         return remote(w_h.at[pl.ds(pl.multiple_of(core * half, half), half),
                              pl.ds(pl.multiple_of(peer[1] * OUT, OUT), OUT)],
-                      half_rows(t, core), w_s.at[n], w_r.at[t], peer)
+                      half_rows(t, core), w_s.at[0], w_r.at[t], peer)
     for n in range(7):
         w_copy(n).start()
 
@@ -177,32 +183,26 @@
 
     own_kv.wait()
 
-    def wait_kv(i, _):
-        d = (c + SHARDS - i) % SHARDS
-        remote(skv.at[0, pl.ds(0, BLK)], rkv.at[at16(d * BLK, BLK)], kv_s.at[d], kv_r.at[d],
-               (d, t)).wait_recv()
-        return 0
-    lax.fori_loop(1, SHARDS, wait_kv, 0)
+    rest = (SHARDS - 1) * BLK
+    landed(rkv.at[pl.ds(0, rest)], kv_r.at[0])
     mine = jnp.dot(unp[...], rkv[...], preferred_element_type=F32).astype(BF)
-    for lv in range(CHIPS):
-        kv[core, lv, j] = mine[lv * BLK:(lv + 1) * BLK]
-
-    sent = []
+    kv[core, j] = mine.reshape(CHIPS, BLK, HD)
+
+    count = [0] * 4
     ways = [(ctx_of(xl, (z + 1) % 8, core), t), (ctx_of(xl, (z + 7) % 8, core), t), (cx, t), (mate, t)]
     RIGHT, LEFT, CROSS, DIE = range(4)
 
     def piece(g, b):
-        return kv.at[core, pl.ds(g * QL, QL), b]
+        return kv.at[core, b, pl.ds(g * QL, QL)]
 
     def go(g, b, *to):
         for way in to:
-            rsem = die_r.at[g, b] if way == DIE else ring_r.at[g, b]
-            cp = remote(piece(g, b), piece(g, b), ring_s.at[way, g, b], rsem, ways[way])
-            cp.start()
-            sent.append(cp)
+            rsem = die_r.at[g] if way == DIE else ring_r.at[g, b]
+            remote(piece(g, b), piece(g, b), ring_s.at[way], rsem, ways[way]).start()
+            count[way] += 1
 
     def arrive(g, b, *to):
-        remote(piece(g, b), piece(g, b), ring_s.at[0, g, b], ring_r.at[g, b], (mate, t)).wait_recv()
+        landed(piece(g, b), ring_r.at[g, b])
         go(g, b, *to)
 
     def same(d):
@@ -211,35 +211,23 @@
     def other(d):
         return (1 - xl) * 8 + (z + 8 + d) % 8
 
+    routes = [(3, 4, 2, 1), (4, 3, 0, 1)]
+
     def tick(g, k):
+        own_r, own_l, far_r, far_l = routes[g % 2]
         if k == 0:
             go(g, j, RIGHT, LEFT, CROSS, DIE)
-        elif k == 1:
-            arrive(g, other(0), RIGHT, LEFT, DIE)
-            arrive(g, same(-1), RIGHT, DIE)
-            arrive(g, same(1), LEFT, DIE)
-        elif k == 2:
-            arrive(g, other(-1), RIGHT, DIE)
-            arrive(g, other(1), DIE)
-            arrive(g, same(-2), RIGHT, DIE)
-            arrive(g, same(2), LEFT, CROSS, DIE)
-        elif k == 3:
-            arrive(g, other(-2), DIE)
-            arrive(g, same(-3), CROSS, DIE)
-            arrive(g, same(3), LEFT, CROSS, DIE)
-            arrive(g, other(2), DIE)
-        else:
-            arrive(g, same(4), CROSS, DIE)
-            arrive(g, other(-3), DIE)
-            arrive(g, other(3), DIE)
-            arrive(g, other(4), DIE)
+        if k == 1:
+            arrive(g, other(0), *([RIGHT] * (far_r > 0) + [LEFT] * (far_l > 0) + [DIE]))
+        for d, way, hops, far in ((-k, RIGHT, own_r, far_r), (k, LEFT, own_l, far_l)):
+            if 1 <= k <= hops:
+                arrive(g, same(d), *([way] * (k < hops) + [CROSS] * (k > far) + [DIE]))
+        for d, way, hops, far in ((1 - k, RIGHT, own_r, far_r), (k - 1, LEFT, own_l, far_l)):
+            if 1 <= k - 1 <= hops:
+                arrive(g, other(d), *([way] * (k - 1 < far) + [DIE]))
 
     def whole(g):
-        def wait_die(b, _):
-            ref = kv.at[1 - core, pl.ds(g * QL, QL), b]
-            remote(ref, ref, ring_s.at[0, g, b], die_r.at[g, b], (mate, t)).wait_recv()
-            return 0
-        lax.fori_loop(0, CHIPS, wait_die, 0)
+        landed(kv.at[1 - core, :, pl.ds(g * QL, QL)], die_r.at[g])
 
     def update(r0, n, s, vals):
         rows = pl.ds(r0, n)
@@ -255,22 +243,19 @@
         r0 = b * QROWS
         if b > g:
             n = QROWS // 2
-
-            @pl.loop(0, QL * ROWS // KC)
-            def _(i):
-                lv = pl.ds(g * QL + i * (KC // ROWS), KC // ROWS)
-                kk = kv[0, lv].reshape(KC, HD)
-                vv = kv[1, lv].reshape(KC, HD)
-                ss = [lax.dot_general(qs[r0 + h * n:r0 + (h + 1) * n, :], kk, NT, preferred_element_type=F32)
-                      for h in range(2)]
-                for h in range(2):
-                    update(r0 + h * n, n, ss[h], vv)
+            lv = slice(g * QL, (g + 1) * QL)
+            kk = kv[0, :, lv].reshape(QL * ROWS, HD)
+            vv = kv[1, :, lv].reshape(QL * ROWS, HD)
+            ss = [lax.dot_general(qs[r0 + h * n:r0 + (h + 1) * n, :], kk, NT, preferred_element_type=F32)
+                  for h in range(2)]
+            for h in range(2):
+                update(r0 + h * n, n, ss[h], vv)
             return
         for i in range(QL):
             lv = g * QL + i
             rs, n = r0 + i * LROWS, QROWS - i * LROWS
-            kk = kv[0, lv].reshape(ROWS, HD)
-            vv = kv[1, lv].reshape(ROWS, HD)
+            kk = kv[0, :, lv].reshape(ROWS, HD)
+            vv = kv[1, :, lv].reshape(ROWS, HD)
             s = lax.dot_general(qs[rs:rs + n, :], kk, NT, preferred_element_type=F32)
             r = lax.broadcasted_iota(jnp.int32, (LROWS, ROWS), 0)
             lim = jnp.where(r >= BLK, r - BLK, r) + j * BLK
@@ -279,13 +264,11 @@
             s = top if n == LROWS else jnp.concatenate([top, s[LROWS:]], axis=0)
             update(rs, n, s, vv)
 
-    slot_a = z * 2 + core
-
     def here(h):
         return af.at[t, at16(z * BLK, BLK), pl.ds(pl.multiple_of(core * 256 + h * HD, HD), HD)]
 
     def o_copy(lv, h):
-        return remote(o_s.at[pl.ds(lv * LROWS + h * BLK, BLK)], here(h), a_s.at[lv, h], a_r.at[slot_a, h],
+        return remote(o_s.at[pl.ds(lv * LROWS + h * BLK, BLK)], here(h), a_s.at[0], a_r.at[0],
                       (2 * lv + xl, t))
 
     def o_own(lv, h):
@@ -307,13 +290,7 @@
 
     def take_queries():
         own_q.wait()
-
-        def wait_q(i, _):
-            e = (c + SHARDS - i) % SHARDS
-            remote(sq.at[0, pl.ds(0, BLK)], rq.at[at16(e * BLK, BLK)], q_s.at[e], q_r.at[e],
-                   (e, t)).wait_recv()
-            return 0
-        lax.fori_loop(1, SHARDS, wait_q, 0)
+        landed(rq.at[pl.ds(0, rest)], q_r.at[0])
         r = jnp.dot(unp[...], rq[...], preferred_element_type=F32).astype(BF)
         for lv in range(CHIPS):
             for h in range(2):
@@ -322,60 +299,53 @@
 
     work = {g: [(g, b) for b in range(g, GROUPS)] for g in range(GROUPS)}
     ready, todo = 0, []
-    for step in range(3 * (GROUPS - 1) + 5):
+    for step in range(STAGGER * (GROUPS - 1) + 6):
         for g in range(GROUPS):
-            if 0 <= step - 3 * g <= 4:
-                tick(g, step - 3 * g)
+            if 0 <= step - STAGGER * g <= 5:
+                tick(g, step - STAGGER * g)
         if step == 4:
             take_queries()
-        if step - 3 * ready == 4:
+        if step - STAGGER * ready == 5:
             whole(ready)
             todo += work[ready]
             ready += 1
-        for _ in range(1 if ready < GROUPS else len(todo)):
+        for _ in range(2 if ready < GROUPS else len(todo)):
             if todo:
                 g, b = todo.pop(0)
                 unit(g, b)
                 if g == b:
                     finish(b)
 
-    passed = []
     for n in range(7):
         b = w_peers[n][1]
-        remote(half_rows(b, core), half_rows(b, core), w_s.at[n], w_r.at[b], (mate, t)).wait_recv()
-        cp = remote(half_rows(b, core), half_rows(b, core), wd_s.at[n], wd_r.at[b], (mate, t))
-        cp.start()
-        passed.append(cp)
+        landed(half_rows(b, core), w_r.at[b])
+        remote(half_rows(b, core), half_rows(b, core), wd_s.at[0], wd_r.at[b], (mate, t)).start()
     loads["w"].wait()
 
-    for n in range(CHIPS):
-        src = ctx_of(core, n // 2, n % 2)
-        for h in range(2):
-            ref = af.at[t, pl.ds((n // 2) * BLK, BLK), pl.ds((n % 2) * 256 + h * HD, HD)]
-
-            @pl.when(src != c)
-            def _():
-                remote(o_s.at[pl.ds(0, BLK)], ref, a_s.at[n, h], a_r.at[n, h], (mate, t)).wait_recv()
-
-            @pl.when(src == c)
-            def _():
-                o_own(0, h).wait()
+    mixed = xl == core
+
+    @pl.when(mixed)
+    def _():
+        o_own(0, 0).wait()
+        o_own(0, 1).wait()
+        landed(o_s.at[pl.ds(0, 15 * LROWS)], a_r.at[0])
+
+    @pl.when(jnp.logical_not(mixed))
+    def _():
+        landed(o_s, a_r.at[0])
 
     def pass_on(b, *to):
         for way in to:
-            cp = remote(af.at[b], af.at[b], g_s.at[way, b], g_r.at[b], gat[way])
-            cp.start()
-            sent.append(cp)
+            remote(af.at[b], af.at[b], g_s.at[0], g_r.at[b], gat[way]).start()
 
     def got(b, *to):
-        remote(af.at[b], af.at[b], g_s.at[0, b], g_r.at[b], (mate, t)).wait_recv()
+        landed(af.at[b], g_r.at[b])
         pass_on(b, *to)
 
     def mul(b, begin=False):
         rows = pl.ds(pl.multiple_of(b * 512, 512), 512)
         if not begin:
-            ref = half_rows(b, 1 - core)
-            remote(ref, ref, wd_s.at[0], wd_r.at[b], (mate, t)).wait_recv()
+            landed(half_rows(b, 1 - core), wd_r.at[b])
 
         @pl.loop(0, OUT // 256)
         def _(n):
@@ -403,22 +373,22 @@
     mul(opp * 2 + 1 - xh)
     out[...] = po[...].astype(BF)
 
-    for cp in passed + sent:
-        cp.wait_send()
-    for n in range(7):
-        w_copy(n).wait_send()
-    for lv in range(CHIPS):
-        @pl.when(2 * lv + xl != c)
-        def _():
-            o_copy(lv, 0).wait_send()
-            o_copy(lv, 1).wait_send()
-
-    def wait_sends(i, _):
-        d = (c + i) % SHARDS
-        kv_copy(d).wait_send()
-        q_copy(d).wait_send()
-        return 0
-    lax.fori_loop(1, SHARDS, wait_sends, 0)
+    left(af.at[pl.ds(0, 7)], g_s.at[0])
+    left(wf.at[pl.ds(0, 7 * half)], w_s.at[0])
+    left(wf.at[pl.ds(0, 7 * half)], wd_s.at[0])
+    for way in range(4):
+        parts = 1 if count[way] % 4 == 0 else 2
+        left(kv.at[0, pl.ds(0, parts * count[way] // 4), pl.ds(0, CHIPS // parts)], ring_s.at[way])
+
+    @pl.when(mixed)
+    def _():
+        left(o_s.at[pl.ds(0, 15 * LROWS)], a_s.at[0])
+
+    @pl.when(jnp.logical_not(mixed))
+    def _():
+        left(o_s, a_s.at[0])
+    left(rkv.at[pl.ds(0, rest)], kv_s.at[0])
+    left(rq.at[pl.ds(0, rest)], q_s.at[0])
 
 
 def local(query, key, value, keep_rank, kept_count, out_weight):
@@ -438,10 +408,10 @@
             VMEM((2 * ROWS, HD), BF), VMEM((2, CHIPS, CHIPS, BLK, HD), BF),
             VMEM((2 * ROWS, HD), F32), VMEM((2 * ROWS, 2 * HD), F32), VMEM((2 * ROWS, HD), BF),
             VMEM((8, 384, 512), BF), VMEM((4096, OUT), BF), VMEM((384, OUT), F32),
-            dma((12,)), dma((SHARDS,)), dma((SHARDS,)), dma((SHARDS,)), dma((SHARDS,)),
-            dma((4, GROUPS, CHIPS)), dma((GROUPS, CHIPS)), dma((GROUPS, CHIPS)),
-            dma((8,)), dma((8,)), dma((8,)), dma((8,)),
-            dma((CHIPS, 2)), dma((CHIPS, 2)), dma((3, 8)), dma((8,)),
+            dma((12,)), dma((1,)), dma((1,)), dma((1,)), dma((1,)),
+            dma((4,)), dma((GROUPS, CHIPS)), dma((GROUPS,)),
+            dma((1,)), dma((8,)), dma((1,)), dma((8,)),
+            dma((1,)), dma((1,)), dma((1,)), dma((8,)),
         ],
         compiler_params=pltpu.CompilerParams(
             collective_id=0, has_side_effects=True, vmem_limit_bytes=56 << 20),

time: 148 us -> 118 us (0.80)
  Pallas kernels: 146 us -> 115 us
    pallas_call x1, Pallas kernels: 146 us -> 115 us  [local(): pl.pallas_call(layer_kernel, out_shape=jax.ShapeDtypeStruct((384, OUT), B...]
where the time goes in v3:
time: 118 us; the launch traced here: 117 us
  Pallas kernels  115 us (97%)
  local copies, waits for them, and re-layouts  2.06 us (2%)
    pallas_call x1, Pallas kernels, local(): pl.pallas_call(layer_kernel, out_shape=jax.ShapeDtypeStruct((384, OUT), B...  115 us

profile of v3, /device:TPU:1, one launch (start us, length us, event | category | flops | bytes accessed | tf_op | source)
XLA Modules:
  0.0 117.1 jit_solution(1990906282846621267)
XLA Ops:
  0.0 115.0 %layer.1 = bf16[384,1024]{1,0:T(8,128)(2,1)} custom-call(s32[32]{0:T(128)} %cnt.1, s32[1,768]{1,0:T(1,128)} %rank_h.1, bf16[768,512]{1,0:T(8,128)(2,1)} %q_h.1, bf16[768,128]{1,0:T(8,128)(2,1)} %k_h.1, bf16[768,128]{1,0:T(8,128)(2,1)} %v_h.1, f32[2,768,128]{2,1,0:T(8,128)} %constant.6.clone.own_h, f32[2,32,128]{2,1,0:T(8,128)} %constant.7.clone.base_h, ...), custom_call_target="tpu_custom_call" | custom-call | flops 12999999488 | bytes 12582912 | tf_op jit(solution)/shard_map/layer/pallas_call | solution.py:398
  115.0 2.1 %copy.11 = bf16[384,1024]{1,0:T(8,128)(2,1)} copy(bf16[384,1024]{1,0:T(8,128)(2,1)} %layer.1) | data formatting | bytes 1572864

commit v4 on v3

--- a/solution.py
+++ b/solution.py
@@ -16,9 +16,8 @@
 SLOTS = SHARDS * BLK
 QL = 4
 GROUPS = CHIPS // QL
-LROWS = 2 * BLK
-QROWS = QL * LROWS
-STAGGER = 1
+QROWS = QL * BLK
+SECOND = 6
 OUT = 1024
 NT = (((1,), (1,)), ((), ()))
 MESH = pl.DeviceIdType.MESH
@@ -74,7 +73,8 @@
     for n, (name, src, dst) in enumerate([
             ("rank", rank_h, rank), ("k", k_h, kin), ("own", own_h, own), ("base", base_h, base),
             ("v", v_h, vin), ("q", q_h, qin), ("cols", cols_h, cols),
-            ("w", w_h.at[:, wcol], wf.at[pl.ds(pl.multiple_of(t * 512, 512), 512)])]):
+            *[(f"w{n}", w_h.at[pl.ds(n * 128, 128), wcol],
+               wf.at[n % 2, pl.ds(pl.multiple_of(t * 256 + n // 2 * 128, 128), 128)]) for n in range(4)]]):
         loads[name] = pltpu.make_async_copy(src, dst, ld.at[n])
         loads[name].start()
 
@@ -127,44 +127,47 @@
         return remote(skv.at[d % 2, at16((d // 2) * BLK, BLK)], rkv.at[at16(c * BLK, BLK)],
                       kv_s.at[0], kv_r.at[0], (d, t))
 
-    def q_copy(d):
-        return remote(sq.at[d % 2, at16((d // 2) * BLK, BLK)], rq.at[at16(c * BLK, BLK)],
-                      q_s.at[0], q_r.at[0], (d, t))
+    def q_copy(d, h):
+        return remote(sq.at[2 * (d % 2) + h, at16((d // 2) * BLK, BLK)], rq.at[h, at16(c * BLK, BLK)],
+                      q_s.at[h], q_r.at[h], (d, t))
 
     def start_kv(i, _):
         kv_copy((c + i) % SHARDS).start()
         return 0
     lax.fori_loop(1, SHARDS, start_kv, 0)
-    own_kv = pltpu.make_async_copy(skv.at[core, at16(j * BLK, BLK)], rkv.at[at16(c * BLK, BLK)], ld.at[8])
+    own_kv = pltpu.make_async_copy(skv.at[core, at16(j * BLK, BLK)], rkv.at[at16(c * BLK, BLK)], ld.at[11])
     own_kv.start()
 
-    half = 256
-
-    def half_rows(b, cr):
-        return wf.at[pl.ds(pl.multiple_of(b * 512 + cr * half, half), half)]
-
-    def w_copy(n):
+    def half_rows(h, b, cr):
+        return wf.at[h, pl.ds(pl.multiple_of(b * 256 + cr * 128, 128), 128)]
+
+    def w_copy(n, h):
         peer = w_peers[n]
-        return remote(w_h.at[pl.ds(pl.multiple_of(core * half, half), half),
+        return remote(w_h.at[pl.ds(pl.multiple_of(core * 256 + h * 128, 128), 128),
                              pl.ds(pl.multiple_of(peer[1] * OUT, OUT), OUT)],
-                      half_rows(t, core), w_s.at[0], w_r.at[t], peer)
+                      half_rows(h, t, core), w_s.at[0], w_r.at[t], peer)
     for n in range(7):
-        w_copy(n).start()
+        w_copy(n, 0).start()
+        w_copy(n, 1).start()
 
     scale = math.log2(math.e) / math.sqrt(HD)
     loads["q"].wait()
     for h in range(4):
         xs[:, h * HD:(h + 1) * HD] = rotate(qin[:, h * HD:(h + 1) * HD], scale)
     qp = jnp.dot(perm, xs[:, :4 * HD], preferred_element_type=F32).astype(BF)
-    sq[0] = qp[:, :2 * HD]
-    sq[1] = qp[:, 2 * HD:]
-
-    def start_q(i, _):
-        q_copy((c + i) % SHARDS).start()
-        return 0
-    lax.fori_loop(1, SHARDS, start_q, 0)
-    own_q = pltpu.make_async_copy(sq.at[core, at16(j * BLK, BLK)], rq.at[at16(c * BLK, BLK)], ld.at[9])
-    own_q.start()
+    for h in range(4):
+        sq[h] = qp[:, h * HD:(h + 1) * HD]
+
+    def send_queries(h):
+        def start_q(i, _):
+            q_copy((c + i) % SHARDS, h).start()
+            return 0
+        lax.fori_loop(1, SHARDS, start_q, 0)
+    own_q = [pltpu.make_async_copy(sq.at[2 * core + h, at16(j * BLK, BLK)], rq.at[h, at16(c * BLK, BLK)],
+                                   ld.at[12 + h]) for h in range(2)]
+    own_q[0].start()
+    own_q[1].start()
+    send_queries(0)
 
     loads["cols"].wait()
     grp, mod = cols[0:1, :], cols[1:2, :]
@@ -239,156 +242,157 @@
         vo = jnp.concatenate([vals, jnp.ones(vals.shape, BF)], axis=1)
         acc_s[rows, :] = acc_s[rows, :] * jnp.tile(a, (1, 2)) + jnp.dot(p, vo, preferred_element_type=F32)
 
-    def unit(g, b):
-        r0 = b * QROWS
-        if b > g:
-            n = QROWS // 2
-            lv = slice(g * QL, (g + 1) * QL)
-            kk = kv[0, :, lv].reshape(QL * ROWS, HD)
-            vv = kv[1, :, lv].reshape(QL * ROWS, HD)
-            ss = [lax.dot_general(qs[r0 + h * n:r0 + (h + 1) * n, :], kk, NT, preferred_element_type=F32)
-                  for h in range(2)]
-            for h in range(2):
-                update(r0 + h * n, n, ss[h], vv)
-            return
+    def unit(g, h):
+        lv = slice(g * QL, (g + 1) * QL)
+        kk = kv[0, :, lv].reshape(QL * ROWS, HD)
+        vv = kv[1, :, lv].reshape(QL * ROWS, HD)
+        later = range(g + 1, GROUPS)
+        ss = [lax.dot_general(qs[h, b * QROWS:(b + 1) * QROWS, :], kk, NT, preferred_element_type=F32)
+              for b in later]
+        for b, s in zip(later, ss):
+            update(h * ROWS + b * QROWS, QROWS, s, vv)
         for i in range(QL):
             lv = g * QL + i
-            rs, n = r0 + i * LROWS, QROWS - i * LROWS
+            rs, n = lv * BLK, QROWS - i * BLK
             kk = kv[0, :, lv].reshape(ROWS, HD)
             vv = kv[1, :, lv].reshape(ROWS, HD)
-            s = lax.dot_general(qs[rs:rs + n, :], kk, NT, preferred_element_type=F32)
-            r = lax.broadcasted_iota(jnp.int32, (LROWS, ROWS), 0)
-            lim = jnp.where(r >= BLK, r - BLK, r) + j * BLK
-            col = lax.broadcasted_iota(jnp.int32, (LROWS, ROWS), 1)
-            top = jnp.where(col <= lim, s[:LROWS], -1e30)
-            s = top if n == LROWS else jnp.concatenate([top, s[LROWS:]], axis=0)
-            update(rs, n, s, vv)
+            s = lax.dot_general(qs[h, rs:rs + n, :], kk, NT, preferred_element_type=F32)
+            lim = lax.broadcasted_iota(jnp.int32, (BLK, ROWS), 0) + j * BLK
+            col = lax.broadcasted_iota(jnp.int32, (BLK, ROWS), 1)
+            top = jnp.where(col <= lim, s[:BLK], -1e30)
+            s = top if n == BLK else jnp.concatenate([top, s[BLK:]], axis=0)
+            update(h * ROWS + rs, n, s, vv)
+        finish(g, h)
 
     def here(h):
-        return af.at[t, at16(z * BLK, BLK), pl.ds(pl.multiple_of(core * 256 + h * HD, HD), HD)]
+        return af.at[h, t, at16(z * BLK, BLK), pl.ds(pl.multiple_of(core * HD, HD), HD)]
 
     def o_copy(lv, h):
-        return remote(o_s.at[pl.ds(lv * LROWS + h * BLK, BLK)], here(h), a_s.at[0], a_r.at[0],
-                      (2 * lv + xl, t))
+        return remote(o_s.at[h, pl.ds(lv * BLK, BLK)], here(h), a_s.at[h], a_r.at[h], (2 * lv + xl, t))
 
     def o_own(lv, h):
-        return pltpu.make_async_copy(o_s.at[pl.ds(lv * LROWS + h * BLK, BLK)], here(h), ld.at[10 + h])
-
-    def finish(b):
-        rows = pl.ds(b * QROWS, QROWS)
-        o_s[rows, :] = (acc_s[rows, :HD] / acc_s[rows, HD:]).astype(BF)
+        return pltpu.make_async_copy(o_s.at[h, pl.ds(lv * BLK, BLK)], here(h), ld.at[14 + h])
+
+    def finish(b, h):
+        rows = pl.ds(h * ROWS + b * QROWS, QROWS)
+        o_s[h, pl.ds(b * QROWS, QROWS), :] = (acc_s[rows, :HD] / acc_s[rows, HD:]).astype(BF)
         for lv in range(b * QL, (b + 1) * QL):
             @pl.when(2 * lv + xl != c)
             def _():
-                o_copy(lv, 0).start()
-                o_copy(lv, 1).start()
+                o_copy(lv, h).start()
 
             @pl.when(2 * lv + xl == c)
             def _():
-                o_own(lv, 0).start()
-                o_own(lv, 1).start()
-
-    def take_queries():
-        own_q.wait()
-        landed(rq.at[pl.ds(0, rest)], q_r.at[0])
-        r = jnp.dot(unp[...], rq[...], preferred_element_type=F32).astype(BF)
-        for lv in range(CHIPS):
-            for h in range(2):
-                qs[lv * LROWS + h * BLK:lv * LROWS + (h + 1) * BLK, :] = r[
-                    lv * BLK:(lv + 1) * BLK, h * HD:(h + 1) * HD]
-
-    work = {g: [(g, b) for b in range(g, GROUPS)] for g in range(GROUPS)}
-    ready, todo = 0, []
-    for step in range(STAGGER * (GROUPS - 1) + 6):
+                o_own(lv, h).start()
+
+    mixed = xl == core
+
+    def take_rows(h):
+        @pl.when(mixed)
+        def _():
+            o_own(0, h).wait()
+            landed(o_s.at[h, pl.ds(0, 15 * BLK)], a_r.at[h])
+
+        @pl.when(jnp.logical_not(mixed))
+        def _():
+            landed(o_s.at[h], a_r.at[h])
+
+    def take_queries(h):
+        own_q[h].wait()
+        landed(rq.at[h, pl.ds(0, rest)], q_r.at[h])
+        qs[h] = jnp.dot(unp[...], rq[h], preferred_element_type=F32).astype(BF)
+
+    for step in range(GROUPS + 5):
         for g in range(GROUPS):
-            if 0 <= step - STAGGER * g <= 5:
-                tick(g, step - STAGGER * g)
+            if 0 <= step - g <= 5:
+                tick(g, step - g)
+        if step == SECOND:
+            send_queries(1)
         if step == 4:
-            take_queries()
-        if step - STAGGER * ready == 5:
-            whole(ready)
-            todo += work[ready]
-            ready += 1
-        for _ in range(2 if ready < GROUPS else len(todo)):
-            if todo:
-                g, b = todo.pop(0)
-                unit(g, b)
-                if g == b:
-                    finish(b)
-
-    for n in range(7):
-        b = w_peers[n][1]
-        landed(half_rows(b, core), w_r.at[b])
-        remote(half_rows(b, core), half_rows(b, core), wd_s.at[0], wd_r.at[b], (mate, t)).start()
-    loads["w"].wait()
-
-    mixed = xl == core
-
-    @pl.when(mixed)
-    def _():
-        o_own(0, 0).wait()
-        o_own(0, 1).wait()
-        landed(o_s.at[pl.ds(0, 15 * LROWS)], a_r.at[0])
-
-    @pl.when(jnp.logical_not(mixed))
-    def _():
-        landed(o_s, a_r.at[0])
-
-    def pass_on(b, *to):
+            take_queries(0)
+        if step >= 5:
+            whole(step - 5)
+            unit(step - 5, 0)
+
+    def pass_on(h, b, *to):
         for way in to:
-            remote(af.at[b], af.at[b], g_s.at[0], g_r.at[b], gat[way]).start()
-
-    def got(b, *to):
-        landed(af.at[b], g_r.at[b])
-        pass_on(b, *to)
-
-    def mul(b, begin=False):
-        rows = pl.ds(pl.multiple_of(b * 512, 512), 512)
-        if not begin:
-            landed(half_rows(b, 1 - core), wd_r.at[b])
+            remote(af.at[h, b], af.at[h, b], g_s.at[0], g_r.at[h, b], gat[way]).start()
+
+    def got(h, b, *to):
+        landed(af.at[h, b], g_r.at[h, b])
+        pass_on(h, b, *to)
+
+    def mul(h, b, begin=False):
+        rows = pl.ds(pl.multiple_of(b * 256, 256), 256)
+        if h == 0 and not begin:
+            landed(wf.at[0, pl.ds(0, 256)], wd_r.at[b])
 
         @pl.loop(0, OUT // 256)
         def _(n):
             cs = pl.ds(pl.multiple_of(n * 256, 256), 256)
-            part = jnp.dot(af[b], wf[rows, cs], preferred_element_type=F32)
+            part = jnp.dot(af[h, b], wf[h, rows, cs], preferred_element_type=F32)
             po[:, cs] = part if begin else po[:, cs] + part
 
-    lo, hi, opp = (y + 3) % 4, (y + 1) % 4, (y + 2) % 4
-    pass_on(t, 0, 1, 2)
-    mul(t, True)
-    bx = y * 2 + 1 - xh
-    got(bx, 1, 2)
-    got(lo * 2 + xh, 1)
-    mul(bx)
-    mul(lo * 2 + xh)
-    got(hi * 2 + xh)
-    mul(hi * 2 + xh)
-    got(hi * 2 + 1 - xh, 2)
-    mul(hi * 2 + 1 - xh)
-    got(lo * 2 + 1 - xh)
-    mul(lo * 2 + 1 - xh)
-    got(opp * 2 + xh)
-    mul(opp * 2 + xh)
-    got(opp * 2 + 1 - xh)
-    mul(opp * 2 + 1 - xh)
+    lo, hi, opp = (y + 3) % 4 * 2, (y + 1) % 4 * 2, (y + 2) % 4 * 2
+    bx, nx = y * 2 + 1 - xh, 1 - xh
+    take_rows(0)
+    pass_on(0, t, 0, 1, 2)
+    take_queries(1)
+    unit(0, 1)
+    got(0, bx, 1, 2)
+    got(0, lo + xh, 1)
+    unit(1, 1)
+    got(0, hi + xh)
+    got(0, hi + nx, 2)
+    unit(2, 1)
+    unit(3, 1)
+    for n in range(7):
+        b = w_peers[n][1]
+        landed(wf.at[0, pl.ds(0, 256)], w_r.at[b])
+        for h in range(2):
+            remote(half_rows(h, b, core), half_rows(h, b, core), wd_s.at[0], wd_r.at[b], (mate, t)).start()
+    for n in range(4):
+        loads[f"w{n}"].wait()
+
+    mul(0, t, True)
+    mul(0, bx)
+    mul(0, lo + xh)
+    take_rows(1)
+    pass_on(1, t, 0, 1, 2)
+    mul(0, hi + xh)
+    mul(0, hi + nx)
+    for b in (lo + nx, opp + xh, opp + nx):
+        got(0, b)
+        mul(0, b)
+    mul(1, t)
+    got(1, bx, 1, 2)
+    got(1, lo + xh, 1)
+    mul(1, bx)
+    mul(1, lo + xh)
+    got(1, hi + nx, 2)
+    mul(1, hi + nx)
+    for b in (hi + xh, lo + nx, opp + xh, opp + nx):
+        got(1, b)
+        mul(1, b)
     out[...] = po[...].astype(BF)
 
-    left(af.at[pl.ds(0, 7)], g_s.at[0])
-    left(wf.at[pl.ds(0, 7 * half)], w_s.at[0])
-    left(wf.at[pl.ds(0, 7 * half)], wd_s.at[0])
+    left(af.at[:, pl.ds(0, 7)], g_s.at[0])
+    left(wf.at[0, pl.ds(0, 7 * 256)], w_s.at[0])
+    left(wf.at[0, pl.ds(0, 7 * 256)], wd_s.at[0])
     for way in range(4):
         parts = 1 if count[way] % 4 == 0 else 2
         left(kv.at[0, pl.ds(0, parts * count[way] // 4), pl.ds(0, CHIPS // parts)], ring_s.at[way])
-
-    @pl.when(mixed)
-    def _():
-        left(o_s.at[pl.ds(0, 15 * LROWS)], a_s.at[0])
-
-    @pl.when(jnp.logical_not(mixed))
-    def _():
-        left(o_s, a_s.at[0])
+    for h in range(2):
+        left(rq.at[h, pl.ds(0, rest)], q_s.at[h])
+
+        @pl.when(mixed)
+        def _():
+            left(o_s.at[h, pl.ds(0, 15 * BLK)], a_s.at[h])
+
+        @pl.when(jnp.logical_not(mixed))
+        def _():
+            left(o_s.at[h], a_s.at[h])
     left(rkv.at[pl.ds(0, rest)], kv_s.at[0])
-    left(rq.at[pl.ds(0, rest)], q_s.at[0])
 
 
 def local(query, key, value, keep_rank, kept_count, out_weight):
@@ -403,15 +407,15 @@
         scratch_shapes=[
             VMEM((1, ROWS), jnp.int32), VMEM((ROWS, 4 * HD), BF), VMEM((ROWS, HD), BF), VMEM((ROWS, HD), BF),
             VMEM((2, ROWS, HD), F32), VMEM((2, SHARDS, HD), F32), VMEM((8, SLOTS), jnp.int32),
-            VMEM((ROWS, 6 * HD), BF), VMEM((2, ROWS, 2 * HD), BF), VMEM((2, ROWS, HD), BF),
-            VMEM((SLOTS, 2 * HD), BF), VMEM((SLOTS, HD), BF), VMEM((ROWS, SLOTS), BF),
-            VMEM((2 * ROWS, HD), BF), VMEM((2, CHIPS, CHIPS, BLK, HD), BF),
-            VMEM((2 * ROWS, HD), F32), VMEM((2 * ROWS, 2 * HD), F32), VMEM((2 * ROWS, HD), BF),
-            VMEM((8, 384, 512), BF), VMEM((4096, OUT), BF), VMEM((384, OUT), F32),
-            dma((12,)), dma((1,)), dma((1,)), dma((1,)), dma((1,)),
+            VMEM((ROWS, 6 * HD), BF), VMEM((4, ROWS, HD), BF), VMEM((2, ROWS, HD), BF),
+            VMEM((2, SLOTS, HD), BF), VMEM((SLOTS, HD), BF), VMEM((ROWS, SLOTS), BF),
+            VMEM((2, ROWS, HD), BF), VMEM((2, CHIPS, CHIPS, BLK, HD), BF),
+            VMEM((2 * ROWS, HD), F32), VMEM((2 * ROWS, 2 * HD), F32), VMEM((2, ROWS, HD), BF),
+            VMEM((2, 8, 384, 256), BF), VMEM((2, 2048, OUT), BF), VMEM((384, OUT), F32),
+            dma((16,)), dma((1,)), dma((1,)), dma((2,)), dma((2,)),
             dma((4,)), dma((GROUPS, CHIPS)), dma((GROUPS,)),
             dma((1,)), dma((8,)), dma((1,)), dma((8,)),
-            dma((1,)), dma((1,)), dma((1,)), dma((8,)),
+            dma((2,)), dma((2,)), dma((1,)), dma((2, 8)),
         ],
         compiler_params=pltpu.CompilerParams(
             collective_id=0, has_side_effects=True, vmem_limit_bytes=56 << 20),

time: 118 us -> 114 us (0.966)
  Pallas kernels: 115 us -> 112 us
    pallas_call x1, Pallas kernels: 115 us -> 112 us  [local(): pl.pallas_call(layer_kernel, out_shape=jax.ShapeDtypeStruct((384, OUT), B...]
where the time goes in v4:
time: 114 us
  Pallas kernels  112 us (98%)
  local copies, waits for them, and re-layouts  2.06 us (2%)
    pallas_call x1, Pallas kernels, local(): pl.pallas_call(layer_kernel, out_shape=jax.ShapeDtypeStruct((384, OUT), B...  112 us

profile of v4, /device:TPU:1, one launch (start us, length us, event | category | flops | bytes accessed | tf_op | source)
XLA Modules:
  0.0 114.1 jit_solution(9068292456868562577)
XLA Ops:
  0.0 112.1 %layer.1 = bf16[384,1024]{1,0:T(8,128)(2,1)} custom-call(s32[32]{0:T(128)} %cnt.1, s32[1,768]{1,0:T(1,128)} %rank_h.1, bf16[768,512]{1,0:T(8,128)(2,1)} %q_h.1, bf16[768,128]{1,0:T(8,128)(2,1)} %k_h.1, bf16[768,128]{1,0:T(8,128)(2,1)} %v_h.1, f32[2,768,128]{2,1,0:T(8,128)} %constant.6.clone.own_h, f32[2,32,128]{2,1,0:T(8,128)} %constant.7.clone.base_h, ...), custom_call_target="tpu_custom_call" | custom-call | flops 12999999488 | bytes 12582912 | tf_op jit(solution)/shard_map/layer/pallas_call | solution.py:402
  112.1 2.1 %copy.11 = bf16[384,1024]{1,0:T(8,128)(2,1)} copy(bf16[384,1024]{1,0:T(8,128)(2,1)} %layer.1) | data formatting | bytes 1572864
